TPU v7x, 256 devices: a whole 4x4x8 slice. The times are simulated.
256 devices in a mesh: dp: 4 (over x), section: 8 (over z_lo, core), tensor: 8 (over z_hi, y).
Axes of the slice: x: 4, y: 4, z: 8 (z_hi: 2, z_lo: 4; z = z_hi * 4 + z_lo), core: 2. Of those that a mesh axis runs over, the one named last changes fastest.
Arguments:
- states: bfloat16 [16, 512, 8192], P('section', 'dp', 'tensor'), may hold values from -6 to 6
- final_state: bfloat16 [512, 8192], P('dp', 'tensor'), may hold values from -6 to 6
- retained: int32 [8], replicated, may hold values from 0 to 15, as said below
- block_slot: int32 [8], replicated, may hold values from 0 to 7, each once
- w_in: bfloat16 [8, 8192, 4096], P('section', 'tensor', 'dp'), may hold values from -0.0625 to 0.0625
- w_side: bfloat16 [8, 8192, 192], P('section', 'tensor'), may hold values from -0.0234375 to 0.0234375
- w_out: bfloat16 [8, 4096, 8192], P('section', 'dp', 'tensor'), may hold values from -0.09375 to 0.09375
- a_rate: float32 [8, 64], P('section'), may hold values from 0.005 to 0.5
- dt_bias: float32 [8, 64], P('section'), may hold values from -1 to 1
- skip: float32 [8, 64], P('section'), may hold values from -1 to 1
Outputs:
- grad_in: bfloat16 [8, 8192, 4096], P('section', 'tensor', 'dp')
- grad_side: bfloat16 [8, 8192, 192], P('section', 'tensor')
- grad_out: bfloat16 [8, 4096, 8192], P('section', 'dp', 'tensor')
- mean_loss: float32 [8], P('section')
Inputs may be any that keep to these rules, and one draw needn't show every extreme that they name: Distinct layers; layer 0 and layer 15 are always retained.
All inputs are finite; a program needn't handle non-finite values.
Results may differ from a plain program's by a relative error of at most 0.0075.
Values may be sent and summed in bfloat16 or wider, within the bound.
A program may use at most 64 MiB of HBM per device.

v0:
```python
import jax
import jax.numpy as jnp
from jax import lax
from jax.sharding import PartitionSpec as P

P_SIZE = 64
NS = 64


def mixer(values_in, writer, reader, step_raw, biases, rates, skips, seq_count):
    head_count, head_size, token_count = values_in.shape
    seq_len = token_count // seq_count
    step_size = jax.nn.softplus(step_raw + biases[None, :])
    log_decay = -(step_size * rates[None, :])
    log_decay = log_decay.reshape(seq_count, seq_len, head_count).transpose(0, 2, 1)
    cumulative = jnp.cumsum(log_decay, axis=2)
    differences = cumulative[:, :, :, None] - cumulative[:, :, None, :]
    causal = jnp.arange(seq_len)[:, None] >= jnp.arange(seq_len)[None, :]
    decays = jnp.where(causal, jnp.exp(jnp.where(causal, differences, 0.0)), 0.0)
    scores = jnp.einsum(
        "stn,sun->stu",
        reader.reshape(seq_count, seq_len, -1),
        writer.reshape(seq_count, seq_len, -1),
        precision=lax.Precision.HIGHEST,
    )
    weights = decays * scores[:, None]
    values_four = values_in.reshape(head_count, head_size, seq_count, seq_len)
    steps_in = (
        values_four * step_size.reshape(seq_count, seq_len, head_count).transpose(2, 0, 1)[:, None]
    )
    mixed_out = jnp.einsum("shtu,hpsu->hpst", weights, steps_in, precision=lax.Precision.HIGHEST)
    mixed_out = mixed_out + skips[:, None, None, None] * values_four
    return mixed_out.reshape(head_count, head_size, token_count)


def local(states, final_state, retained, block_slot, w_in, w_side, w_out, a_rate, dt_bias, skip):
    section_count = lax.axis_size("section")
    data_count = lax.axis_size("dp")
    tensor_count = lax.axis_size("tensor")
    section_index = lax.axis_index("section")
    data_index = lax.axis_index("dp")
    tensor_index = lax.axis_index("tensor")
    layers_here = states.shape[0]
    feature_cols = states.shape[2]
    block_count = retained.shape[0]
    block_rows = jnp.arange(block_count, dtype=jnp.int32)
    owner_hit = block_slot[None, :] == block_rows[:, None]
    wanted = jnp.sum(jnp.where(owner_hit, retained[None, :], 0), axis=1)
    pair_steps = jnp.arange(2, dtype=jnp.int32)
    is_last = section_index == section_count - 1
    extra = jnp.where(is_last, final_state, jnp.zeros_like(final_state))
    stacked = jnp.concatenate([states, extra[None]], axis=0)
    position = wanted[:, None] + pair_steps[None, :] - section_index * layers_here
    select = (
        position[:, :, None] == jnp.arange(layers_here + 1, dtype=jnp.int32)[None, None, :]
    ).astype(jnp.bfloat16)
    slots = jnp.einsum("jpi,ibf->jpbf", select, stacked, preferred_element_type=jnp.float32).astype(
        jnp.bfloat16
    )
    received = lax.all_to_all(slots, "section", split_axis=0, concat_axis=0, tiled=True)
    pair = jnp.sum(received.astype(jnp.float32), axis=0).astype(jnp.bfloat16)
    source = pair[0]
    target = pair[1]
    gathered = lax.all_gather(source, "dp", axis=0, tiled=True)
    token_count = gathered.shape[0]
    weight_in = w_in[0]
    weight_side = w_side[0]
    weight_out = w_out[0]
    inner_cols = weight_in.shape[1]
    local_cols = inner_cols // tensor_count
    head_count = local_cols // P_SIZE
    piece = weight_in
    values = lax.psum_scatter(
        lax.dot_general(
            piece, gathered, (((0,), (1,)), ((), ())), preferred_element_type=jnp.float32
        ),
        "tensor",
        scatter_dimension=0,
        tiled=True,
    )
    side_part = jnp.dot(gathered, weight_side, preferred_element_type=jnp.float32)
    side = lax.psum(side_part, "tensor")
    head_start = (data_index * tensor_count + tensor_index) * head_count
    step_raw = lax.dynamic_slice_in_dim(side[:, 2 * NS :], head_start, head_count, 1)
    rates = lax.dynamic_slice_in_dim(a_rate[0], head_start, head_count, 0)
    biases = lax.dynamic_slice_in_dim(dt_bias[0], head_start, head_count, 0)
    skips = lax.dynamic_slice_in_dim(skip[0], head_start, head_count, 0)

    def run(values_in, writer, reader, steps_in):
        return mixer(values_in, writer, reader, steps_in, biases, rates, skips, data_count)

    mixed_out, pullback = jax.vjp(
        run,
        values.reshape(head_count, P_SIZE, token_count),
        side[:, :NS],
        side[:, NS : 2 * NS],
        step_raw,
    )
    mixed_b = mixed_out.astype(jnp.bfloat16).reshape(local_cols, token_count)
    block_mixed = lax.all_gather(mixed_b, "tensor", axis=0, tiled=True)
    piece = block_mixed
    output = lax.psum_scatter(
        lax.dot_general(
            piece, weight_out, (((0,), (0,)), ((), ())), preferred_element_type=jnp.float32
        ),
        "dp",
        scatter_dimension=0,
        tiled=True,
    )
    error = output - target.astype(jnp.float32)
    square_sum = lax.psum(jnp.sum(error * error), ("dp", "tensor"))
    mean_loss = square_sum / (token_count * feature_cols * tensor_count)
    out_grad = (2.0 * error / token_count).astype(jnp.bfloat16)
    grad_all = lax.all_gather(out_grad, "dp", axis=0, tiled=True)
    grad_out = jnp.dot(block_mixed, grad_all, preferred_element_type=jnp.float32).astype(
        jnp.bfloat16
    )
    piece = weight_out
    mixed_grad = lax.psum_scatter(
        lax.dot_general(
            piece, grad_all, (((1,), (1,)), ((), ())), preferred_element_type=jnp.float32
        ),
        "tensor",
        scatter_dimension=0,
        tiled=True,
    )
    grad_values, grad_writer, grad_reader, grad_steps = pullback(
        mixed_grad.reshape(head_count, P_SIZE, token_count)
    )
    steps_full = jnp.zeros((token_count, side.shape[1] - 2 * NS), jnp.float32)
    steps_full = lax.dynamic_update_slice_in_dim(steps_full, grad_steps, head_start, 1)
    side_terms = jnp.concatenate([grad_writer, grad_reader, steps_full], axis=1)
    side_grad = lax.psum(side_terms, ("dp", "tensor")).astype(jnp.bfloat16)
    grad_side = lax.dot_general(
        gathered, side_grad, (((0,), (0,)), ((), ())), preferred_element_type=jnp.float32
    ).astype(jnp.bfloat16)
    values_grad = grad_values.astype(jnp.bfloat16).reshape(local_cols, token_count)
    grad_in = lax.dot_general(
        gathered,
        lax.all_gather(values_grad, "tensor", axis=0, tiled=True),
        (((0,), (1,)), ((), ())),
        preferred_element_type=jnp.float32,
    ).astype(jnp.bfloat16)
    return (grad_in[None], grad_side[None], grad_out[None], mean_loss.reshape(1))


def solution(mesh):
    placed = (
        P("section", "dp", "tensor"),
        P("dp", "tensor"),
        P(),
        P(),
        P("section", "tensor", "dp"),
        P("section", "tensor", None),
        P("section", "dp", "tensor"),
        P("section", None),
        P("section", None),
        P("section", None),
    )
    return jax.shard_map(
        local,
        mesh=mesh,
        in_specs=placed,
        out_specs=(
            P("section", "tensor", "dp"),
            P("section", "tensor", None),
            P("section", "dp", "tensor"),
            P("section"),
        ),
        check_vma=False,
    )
```

profile of v0, /device:TPU:32, one launch (start us, length us, event | category | flops | bytes accessed | tf_op | source)
XLA Modules:
  0.0 844.1 jit_solution(6947777881596007950)
XLA Ops:
  7.7 1.6 copy.69
  9.5 1.9 convolution_convert_fusion
  11.3 2.3 copy.71
  13.7 98.0 %all_to_all.5 = bf16[8,2,128,1024]{3,2,1,0:T(8,128)(2,1)} all-to-all(bf16[8,2,128,1024]{3,2,1,0:T(8,128)(2,1)S(1)} %copy.71), channel_id=1, replica_groups=mesh['dp'=4,'section'=8,'tensor'=8] {'section'}, dimensions={0} | all-to-all | bytes 8388608 | tf_op jit(solution)/shard_map/all_to_all | solution.py:60
  111.7 3.2 reduce_sum.69
  115.7 28.8 %all-gather.12.cloned.1.call-done = bf16[1,512,1024]{2,1,0:T(8,128)(2,1)} async-done(((bf16[1,128,1024]{2,1,0:T(8,128)(2,1)}), bf16[1,512,1024]{2,1,0:T(8,128)(2,1)}) %all-gather.12.cloned.1.call-update) | async-done | bytes 1048592 | tf_op jit(solution)/shard_map/all_gather | solution.py:64
  144.5 2.6 fusion.19
  147.2 4.2 fusion.6
  153.3 101.8 %all-reduce.4.cloned.1.call-done = f32[512,192]{0,1:T(8,128)} async-done(((f32[512,192]{0,1:T(8,128)}), f32[512,192]{0,1:T(8,128)}) %all-reduce.4.cloned.1.call-update) | async-done | bytes 393232 | tf_op jit(solution)/shard_map/psum | solution.py:82
  258.6 1.3 fusion.47
  259.9 91.4 %reduce-scatter.4.cloned.1.call-done = f32[128,512]{0,1:T(8,128)} async-done(((f32[1024,512]{0,1:T(8,128)}), f32[128,512]{0,1:T(8,128)}) %reduce-scatter.4.cloned.1.call-update) | async-done | bytes 262160 | tf_op jit(solution)/shard_map/reduce_scatter | solution.py:73
  351.3 2.1 reshape.103
  353.4 1.9 copy.73
  355.3 2.3 fusion.14
  358.5 57.5 %all-gather.6.cloned.1.call-done = bf16[1024,512]{1,0:T(8,128)(2,1)} async-done(((bf16[128,512]{1,0:T(8,128)(2,1)}), bf16[1024,512]{1,0:T(8,128)(2,1)}) %all-gather.6.cloned.1.call-update) | async-done | bytes 1048592 | tf_op jit(solution)/shard_map/all_gather | solution.py:100
  416.0 3.8 fusion.2
  419.9 28.8 %reduce-scatter.6.cloned.1.call-done = f32[128,1024]{1,0:T(8,128)} async-done(((f32[512,1024]{1,0:T(8,128)}), f32[128,1024]{1,0:T(8,128)}) %reduce-scatter.6.cloned.1.call-update) | async-done | bytes 524304 | tf_op jit(solution)/shard_map/reduce_scatter | solution.py:102
  448.7 2.6 multiply_reduce_fusion
  451.4 26.4 %all-gather.8.cloned.1.call-done = bf16[512,1024]{1,0:T(8,128)(2,1)} async-done(((bf16[128,1024]{1,0:T(8,128)(2,1)}), bf16[512,1024]{1,0:T(8,128)(2,1)}) %all-gather.8.cloned.1.call-update) | async-done | bytes 1048592 | tf_op jit(solution)/shard_map/all_gather | solution.py:114
  477.7 3.8 fusion.9
  481.8 96.3 %reduce-scatter.8.cloned.1.call-done = f32[128,512]{0,1:T(8,128)} async-done(((f32[1024,512]{0,1:T(8,128)}), f32[128,512]{0,1:T(8,128)}) %reduce-scatter.8.cloned.1.call-update) | async-done | bytes 262160 | tf_op jit(solution)/shard_map/reduce_scatter | solution.py:119
  578.2 1.8 copy.81
  579.9 1.7 reshape_reshape.7
  581.7 2.6 multiply_reduce_fusion.2
  585.1 4.2 convert_bitcast_fusion
  589.3 1.8 fusion.28
  591.2 5.0 reduce_window_sum.23
  596.2 1.6 convolution_bitcast_fusion.3
  597.8 1.3 convolution_bitcast_fusion.4
  599.9 229.6 %all-reduce.5 = (bf16[512,192]{0,1:T(8,128)(2,1)}, f32[]{:T(128)}) all-reduce(f32[512,192]{0,1:T(8,128)S(1)} %pad_maximum_fusion, f32[]{:T(128)} %get-tuple-element.11), channel_id=1, replica_groups=mesh['dp'=4,'section'=8,'tensor'=8] {'dp','tensor'}, use_global_device_ids=true, to_apply=%region_12.13 | all-reduce | flops 98305 | bytes 589832 | tf_op jit(solution)/shard_map/psum | solution.py:133
  830.2 2.1 fusion.12
  832.2 3.8 convert_bitcast_fusion.1
  (77 shorter events, 9.9 us)
Async XLA Ops:
  7.2 408.9 %copy-start = (bf16[1,1024,1024]{2,1,0:T(8,128)(2,1)S(1)}, bf16[1,1024,1024]{2,1,0:T(8,128)(2,1)}, u32[]{:S(2)}) copy-start(bf16[1,1024,1024]{2,1,0:T(8,128)(2,1)} %param.16) | copy-start | bytes 6291460
  7.2 2.1 copy-start.15
  7.2 2.1 copy-start.16
  7.2 137.3 %all-gather.12.cloned.1.call-start = ((), (), s32[]{:S(2)}) async-start(), calls=%async_computation.11 | async-start | bytes 1310720 | tf_op jit(solution)/shard_map/all_gather | solution.py:64
  111.7 32.8 %copy-start.3 = (bf16[1,1024,192]{1,2,0:T(8,128)(2,1)S(1)}, bf16[1,1024,192]{1,2,0:T(8,128)(2,1)}, u32[]{:S(2)}) copy-start(bf16[1,1024,192]{1,2,0:T(8,128)(2,1)} %param.15) | copy-start | bytes 1179652
  114.9 0.9 copy-start.2
  115.7 139.4 %all-reduce.4.cloned.1.call-start = ((), (), s32[]{:S(2)}) async-start(), calls=%async_computation.5 | async-start | bytes 786432 | tf_op jit(solution)/shard_map/psum | solution.py:82
  144.5 2.6 copy-start.1
  147.1 204.2 %reduce-scatter.4.cloned.1.call-start = ((), (), s32[]{:S(2)}) async-start(), calls=%async_computation.4 | async-start | bytes 2359296 | tf_op jit(solution)/shard_map/reduce_scatter | solution.py:73
  151.3 0.7 copy-start.17
  151.3 1.2 copy-start.13
  151.4 1.2 copy-start.14
  151.4 264.6 %all-gather.6.cloned.1.call-start = ((), (), s32[]{:S(2)}) async-start(), calls=%async_computation.6 | async-start | bytes 1179648 | tf_op jit(solution)/shard_map/all_gather | solution.py:100
  152.7 104.2 %copy-start.8 = (f32[2]{0:T(128)}, f32[2]{0:T(128)S(1)}, u32[]{:S(2)}) copy-start(f32[2]{0:T(128)S(1)} %get-tuple-element.19) | copy-start | bytes 28
  258.0 97.3 %copy-start.9 = (f32[4,128,2]{1,0,2:T(4,128)S(1)}, f32[4,128,2]{1,0,2:T(4,128)}, u32[]{:S(2)}) copy-start(f32[4,128,2]{1,0,2:T(4,128)} %reshape.91) | copy-start | bytes 12292
  258.6 96.7 %copy-start.11 = (f32[4,2,128]{2,0,1:T(4,128)S(1)}, f32[4,2,128]{2,0,1:T(4,128)}, u32[]{:S(2)}) copy-start(f32[4,2,128]{2,0,1:T(4,128)} %copy.75) | copy-start | bytes 12292
  358.4 90.3 %reduce-scatter.6.cloned.1.call-start = ((), (), s32[]{:S(2)}) async-start(), calls=%async_computation.7 | async-start | bytes 2621440 | tf_op jit(solution)/shard_map/reduce_scatter | solution.py:102
  419.9 57.9 %all-gather.8.cloned.1.call-start = ((), (), s32[]{:S(2)}) async-start(), calls=%async_computation.8 | async-start | bytes 1310720 | tf_op jit(solution)/shard_map/all_gather | solution.py:114
  451.3 126.8 %reduce-scatter.8.cloned.1.call-start = ((), (), s32[]{:S(2)}) async-start(), calls=%async_computation.9 | async-start | bytes 2359296 | tf_op jit(solution)/shard_map/reduce_scatter | solution.py:119
  481.6 350.6 %all-gather.10.cloned.1.call-start = ((), (), s32[]{:S(2)}) async-start(), calls=%async_computation.10 | async-start | bytes 1179648 | tf_op jit(solution)/shard_map/all_gather | solution.py:140
  585.0 4.2 copy-start.4
  585.0 4.2 copy-start.5
  585.1 4.2 copy-start.6
  585.1 4.2 copy-start.7
  585.1 4.2 copy-start.10
  585.1 4.2 copy-start.12
Sparse Core Ops, SparseCore 0:
  115.8 28.6 all-gather.11
  147.7 107.3 all-reduce.3
  260.3 91.0 reduce-scatter.3
  358.6 57.4 all-gather.5
  420.0 28.6 reduce-scatter.5
  451.4 26.2 all-gather.7
  482.9 95.1 reduce-scatter.7
  585.2 57.4 all-gather.9
where the time goes:
time: 845 us; the launch traced here: 844 us
  waiting for transfers between devices  431 us (51%)
  blocking collectives  328 us (39%)
  matrix products  37.2 us (4%)
  local copies, waits for them, and re-layouts  17.8 us (2%)
  between operations  16.2 us (2%)
  other arithmetic  13.6 us (2%)
    psum x1, blocking collectives, local(): side_grad = lax.psum(side_terms, ('dp', 'tensor')).astype(jnp.bfloat16)  230 us
    psum x1, waiting for transfers between devices, local(): side = lax.psum(side_part, 'tensor')  102 us
    all_to_all x1, blocking collectives, local(): lax.all_to_all(slots, 'section', split_axis=0, concat_axis=0, tiled=True)  98 us
    reduce_scatter x1, waiting for transfers between devices, local(): lax.psum_scatter(lax.dot_general(piece, grad_all, (((1,), (1,)), ((), ())...  96.3 us
    reduce_scatter x1, waiting for transfers between devices, local(): lax.psum_scatter(lax.dot_general(piece, gathered, (((0,), (1,)), ((), ())...  91.4 us
    all_gather x1, waiting for transfers between devices, local(): block_mixed = lax.all_gather(mixed_b, 'tensor', axis=0, tiled=True)  57.5 us
    reduce_scatter x1, waiting for transfers between devices, local(): lax.psum_scatter(lax.dot_general(piece, weight_out, (((0,), (0,)), ((), (...  28.8 us
    all_gather x1, waiting for transfers between devices, local(): gathered = lax.all_gather(source, 'dp', axis=0, tiled=True)  28.8 us
  transfers between devices with their start and end apart: 8, of which 7 were waited for; matrix products, arithmetic and copies ran while one was open for 3% of the time, Pallas kernels for 0%

commit v1 on v0

v1 whole, which is shorter than its diff:
```python
import functools
from types import SimpleNamespace

import jax
import jax.numpy as jnp
from jax import lax
from jax.experimental import pallas as pl
from jax.experimental.pallas import tpu as pltpu
from jax.sharding import PartitionSpec as P

P_SIZE = 64
NS = 64
NZ = 2
MESH = pl.DeviceIdType.MESH
F32 = jnp.float32
BF = jnp.bfloat16
HI = lax.Precision.HIGHEST


def dot(a, b, ca=1, cb=0, precision=None):
    return lax.dot_general(
        a, b, (((ca,), (cb,)), ((), ())), preferred_element_type=F32, precision=precision
    )


def arrival(n):
    return sorted(range(1, n), key=lambda k: min(k, n - k))


def kernel(cfg, stop, states, final, retained, slot, w_in, w_side, w_out, a_rate, dt_bias, skip,
           g_in, g_side, g_out, loss, *scratch):
    b = SimpleNamespace(**dict(zip(cfg.names, scratch)))
    ND, SEC, NY = cfg.nd, cfg.sec, cfg.ny
    T, F, C, H = cfg.t, cfg.f, cfg.c, cfg.c // NZ
    HB, HH = cfg.hb, cfg.hb // NZ
    RC = T // SEC
    SIDE = T + HB
    d, s, t = lax.axis_index("dp"), lax.axis_index("section"), lax.axis_index("tensor")
    zh, y = t // NY, t % NY
    oz = 1 - zh

    def xdev(i):
        return (i, s, t)

    def ydev(i):
        return (d, s, zh * NY + i)

    def sdev(i):
        return (d, i, t)

    zdev = (d, s, oz * NY + y)

    bar = pltpu.get_barrier_semaphore()
    partners = (
        [xdev((d + k) % ND) for k in range(1, ND)]
        + [ydev((y + k) % NY) for k in range(1, NY)]
        + [sdev((s + k) % SEC) for k in range(1, SEC)]
        + [zdev]
    )
    for p in partners:
        pl.semaphore_signal(bar, inc=1, device_id=p, device_id_type=MESH)

    loads = [
        pltpu.make_async_copy(src, dst, b.load_sem.at[i])
        for i, (src, dst) in enumerate((
            (states.at[:, pl.ds(pl.multiple_of(s * RC, 16), RC)], b.layers.at[pl.ds(2 * s, 2)]),
            (w_side.at[0], b.wside), (w_in.at[0], b.win), (w_out.at[0], b.wout), (final, b.final),
        ))
    ]
    for cp in loads:
        cp.start()
    pl.semaphore_wait(bar, len(partners))

    def send(src, dst, sems, i, dev):
        cp = pltpu.make_async_remote_copy(
            src_ref=src, dst_ref=dst, send_sem=sems.at[0, i], recv_sem=sems.at[1, i],
            device_id=dev, device_id_type=MESH,
        )
        return cp

    def rows(i, n=None):
        n = T if n is None else n
        return pl.ds(pl.multiple_of(i * n, 16), n)

    def half(i):
        return pl.ds(pl.multiple_of(i * H, 128), H)

    pending = []

    def go(cp):
        cp.start()
        pending.append(cp)
        return cp

    hop1 = [
        go(send(states.at[:, rows((s + k) % SEC, RC)], b.layers.at[pl.ds(2 * s, 2)], b.h1_sem, k, sdev((s + k) % SEC)))
        for k in range(1, SEC)
    ]
    wanted = []
    for i in range(SEC):
        layer = jnp.int32(0)
        for r in range(SEC):
            layer = layer + jnp.where(slot[r] == i, retained[r], 0)
        wanted.append(layer)
    mine = jnp.int32(0)
    for i in range(SEC):
        mine = mine + jnp.where(s == i, wanted[i], 0)

    def wanted_of(i):
        out = jnp.int32(0)
        for j in range(SEC):
            out = out + jnp.where(i == j, wanted[j], 0)
        return out

    loads[0].wait()
    loads[1].wait()
    heads_all = cfg.heads
    pick = (
        lax.broadcasted_iota(jnp.int32, (HB, heads_all), 1)
        == lax.broadcasted_iota(jnp.int32, (HB, heads_all), 0) + d * HB
    )
    b.wstep[...] = dot(pick.astype(BF), b.wside[:, 2 * NS:], 1, 1).astype(BF)

    for cp in hop1:
        cp.wait_recv()
    hop2 = []
    for k in range(1, SEC):
        to = (s + k) % SEC
        b.stage.at[0, k][...] = b.layers[wanted_of(to)]
        hop2.append(go(send(b.stage.at[0, k], b.src.at[rows(d), :].at[rows(s, RC)], b.h2_sem, k, sdev(to))))
    b.src.at[rows(d), :].at[rows(s, RC)][...] = b.layers[mine]
    hop3 = []
    for k in range(1, SEC):
        to = (s + k) % SEC
        b.stage.at[1, k][...] = b.layers[jnp.minimum(wanted_of(to) + 1, 2 * SEC - 1)]
        hop3.append(go(send(b.stage.at[1, k], b.tgt.at[rows(s, RC)], b.h3_sem, k, sdev(to))))
    b.tgt.at[rows(s, RC)][...] = b.layers[jnp.minimum(mine + 1, 2 * SEC - 1)]
    for cp in hop2:
        cp.wait_recv()

    gather = {
        k: go(send(b.src.at[rows(d)], b.src.at[rows(d)], b.ag_sem, k, xdev((d + k) % ND)))
        for k in arrival(ND)
    }
    loads[2].wait()

    NB = 256

    def product(q, lhs, w, out, rel, transposed=False):
        def step(n, carry):
            cols = pl.ds(pl.multiple_of(n * NB, NB), NB)
            w_n = w[cols, :] if transposed else w[:, cols]
            out.at[rel][:, cols] = dot(lhs[rows(q), :], w_n, 1, 1 if transposed else 0).astype(BF)
            return carry

        lax.fori_loop(0, out.shape[2] // NB, step, 0)

    def c_copies(rel):
        to = ydev((y + rel) % NY)
        return (
            send(b.psend.at[rel], b.prec.at[rel], b.c_sem, rel, to),
            send(b.ssend.at[rel], b.srec.at[rel], b.cs_sem, rel, to),
        )

    for k in [0] + arrival(ND):
        if k:
            gather[k].wait_recv()
        q = (d - k) % ND
        rel = (q - y) % NY
        product(q, b.src, b.win, b.psend, rel)
        b.ssend.at[rel][:T, :] = dot(b.src[rows(q), :], b.wside[:, : 2 * NS]).astype(BF)
        b.ssend.at[rel][T:, :] = dot(b.wstep[...], b.src[rows(q), :], 1, 1).astype(BF)

        @pl.when(rel != 0)
        def _():
            for cp in c_copies(rel):
                cp.start()

    for q in range(ND):
        for j in range(F // 128):
            b.srct[128 * j: 128 * (j + 1), T * q: T * (q + 1)] = (
                b.src[T * q: T * (q + 1), 128 * j: 128 * (j + 1)].T
            )
    for rel in range(1, NY):
        for cp in c_copies(rel):
            cp.wait_recv()
    part = b.psend.at[0][:, half(oz)].astype(F32)
    for rel in range(1, NY):
        part = part + b.prec.at[rel][:, half(oz)].astype(F32)
    b.zsend[...] = part.astype(BF)
    cz = go(send(b.zsend, b.zrec, b.z_sem, 0, zdev))
    part = b.ssend[0].astype(F32)
    for rel in range(1, NY):
        part = part + b.srec[rel].astype(F32)
    b.zssend[...] = part.astype(BF)
    czs = go(send(b.zssend, b.zsrec, b.z_sem, 1, zdev))
    b.side[...] = part
    part = b.psend.at[0][:, half(zh)].astype(F32)
    for rel in range(1, NY):
        part = part + b.prec.at[rel][:, half(zh)].astype(F32)
    cz.wait_recv()
    b.vals[...] = part + b.zrec[...].astype(F32)
    czs.wait_recv()
    b.side[...] += b.zsrec[...].astype(F32)

    head0 = d * HB + zh * HH

    def column(ref):
        at = lax.broadcasted_iota(jnp.int32, (HH, 1), 0)
        out = jnp.zeros((HH, 1), F32)
        for k in range(HH):
            out = jnp.where(at == k, ref[0, head0 + k], out)
        return out

    rate, bias = column(a_rate), column(dt_bias)
    r_t = lax.broadcasted_iota(jnp.int32, (T, T), 0)
    r_u = lax.broadcasted_iota(jnp.int32, (T, T), 1)
    causal = r_t >= r_u
    low = r_u < NS
    raw = b.side[pl.ds(pl.multiple_of(T + zh * HH, 8), HH), :] + bias
    step = jax.nn.softplus(raw)
    cum = dot(-(step * rate), (r_t <= r_u).astype(F32), precision=HI)
    rw = b.side[:T, :]
    wr = pltpu.roll(rw, NS, 1)
    scores = dot(jnp.where(low, wr, 0.0), rw, 1, 1, precision=HI)
    cum_cols = jnp.concatenate([cum] * (T // HH), axis=0).T
    for k in range(HH):
        diff = cum_cols[:, k: k + 1] - cum[k: k + 1, :]
        b.decay[k] = jnp.where(causal, jnp.exp(jnp.where(causal, diff, 0.0)), 0.0)
    for j in range(H // 128):
        cols = slice(128 * j, 128 * (j + 1))
        v = b.vals[:, cols]
        vb = v.astype(BF)
        outs = []
        for k in (2 * j, 2 * j + 1):
            w = (b.decay[k] * scores * step[k: k + 1, :]).astype(BF)
            outs.append(dot(w, vb))
        y2 = jnp.where(low, outs[0], outs[1])
        b.pure[:, cols] = y2
        skips = jnp.where(low, skip[0, head0 + 2 * j], skip[0, head0 + 2 * j + 1])
        b.mhalf[:, cols] = (y2 + skips * v).astype(BF)
    b.mix.at[rows(y)][:, half(zh)] = b.mhalf[...]

    def gather_z(buf, sems):
        return send(b.mhalf if buf is b.mix else b.vghalf, buf.at[rows(y), half(zh)], sems, 0, zdev)

    def gather_y(buf, sems, rel):
        return send(
            b.mhalf if buf is b.mix else b.vghalf, buf.at[rows(y), half(zh)], sems, rel, ydev((y + rel) % NY)
        )

    def forward_y(buf, sems, rel):
        return send(
            buf.at[rows(y), half(oz)], buf.at[rows(y), half(oz)], sems, NY + rel, ydev((y + rel) % NY)
        )

    go(gather_z(b.mix, b.e_sem))
    for rel in arrival(NY):
        go(gather_y(b.mix, b.e_sem, rel))
    gather_z(b.mix, b.e_sem).wait_recv()
    for rel in arrival(NY):
        go(forward_y(b.mix, b.e_sem, rel))
    loads[3].wait()

    def f_copy(rel):
        return send(b.osend.at[rel], b.orec.at[rel], b.f_sem, rel, xdev((d + rel) % ND))

    for k in [0] + arrival(NY):
        if k:
            gather_y(b.mix, b.e_sem, k).wait_recv()
            forward_y(b.mix, b.e_sem, k).wait_recv()
        q = (y - k) % NY
        rel = (q - d) % ND
        product(q, b.mix, b.wout, b.osend, rel)

        @pl.when(rel != 0)
        def _():
            f_copy(rel).start()

    for q in range(NY):
        for j in range(C // 128):
            b.mixt[128 * j: 128 * (j + 1), T * q: T * (q + 1)] = (
                b.mix[T * q: T * (q + 1), 128 * j: 128 * (j + 1)].T
            )
    loads[4].wait()
    for cp in hop3:
        cp.wait_recv()
    inner = mine + 1 < 2 * SEC
    for rel in range(1, ND):
        f_copy(rel).wait_recv()
    total = jnp.zeros((8, 128), F32)
    for j in range(F // 128):
        cols = slice(128 * j, 128 * (j + 1))
        out = b.osend[0, :, cols].astype(F32)
        for rel in range(1, ND):
            out = out + b.orec[rel, :, cols].astype(F32)
        goal = jnp.where(inner, b.tgt[:, cols].astype(F32), b.final[:, cols].astype(F32))
        err = out - goal
        b.ogown[:, cols] = (2.0 * err / (T * ND)).astype(BF)
        total = total + jnp.sum((err * err).reshape(T // 8, 8, 128), axis=0)
    b.og.at[rows(d)][...] = b.ogown[...]
    b.lsum[0] = total

    def h_copy(k):
        return send(b.ogown, b.og.at[rows(d)], b.h_sem, k, xdev((d + k) % ND))

    for k in arrival(ND):
        go(h_copy(k))

    def loss_x(k):
        return send(b.lsum.at[0], b.lrec.at[k], b.l_sem, k, xdev((d + k) % ND))

    def loss_y(k):
        return send(b.lsum.at[1], b.lrec.at[ND + k], b.l_sem, ND + k, ydev((y + k) % NY))

    def loss_z():
        return send(b.lsum.at[2], b.lrec.at[ND + NY], b.l_sem, ND + NY, zdev)

    for k in range(1, ND):
        go(loss_x(k))

    def i_copy(rel):
        return send(b.isend.at[rel], b.irec.at[rel], b.i_sem, rel, ydev((y + rel) % NY))

    for k in [0] + arrival(ND):
        if k:
            h_copy(k).wait_recv()
        q = (d - k) % ND
        rel = (q - y) % NY
        product(q, b.og, b.wout, b.isend, rel, transposed=True)

        @pl.when(rel != 0)
        def _():
            i_copy(rel).start()

    total = b.lsum[0]
    for k in range(1, ND):
        loss_x(k).wait_recv()
        total = total + b.lrec[k]
    b.lsum[1] = total
    for k in range(1, NY):
        go(loss_y(k))
    for rel in range(1, NY):
        i_copy(rel).wait_recv()
    part = b.isend.at[0][:, half(oz)].astype(F32)
    for rel in range(1, NY):
        part = part + b.irec.at[rel][:, half(oz)].astype(F32)
    b.izsend[...] = part.astype(BF)
    iz = go(send(b.izsend, b.izrec, b.z_sem, 2, zdev))

    def store(n, carry):
        at = pl.ds(pl.multiple_of(n * 256, 256), 256)
        b.gout[at, :] = dot(b.mixt[at, :], b.og[...]).astype(BF)
        return carry

    lax.fori_loop(0, C // 256, store, 0)
    out_copy = pltpu.make_async_copy(b.gout, g_out.at[0], b.store_sem.at[0])
    out_copy.start()
    total = b.lsum[1]
    for k in range(1, NY):
        loss_y(k).wait_recv()
        total = total + b.lrec[ND + k]
    b.lsum[2] = total
    go(loss_z())
    iz.wait_recv()

    dscore = jnp.zeros((T, T), F32)
    sums, rowsums = [], []
    at_lane = lax.broadcasted_iota(jnp.int32, (T, 128), 1)
    rowcols = jnp.zeros((T, 128), F32)
    for j in range(H // 128):
        cols = slice(128 * j, 128 * (j + 1))
        own = pl.ds(pl.multiple_of(zh * H + 128 * j, 128), 128)
        g = b.isend.at[0][:, own].astype(F32)
        for rel in range(1, NY):
            g = g + b.irec.at[rel][:, own].astype(F32)
        g = g + b.izrec[:, cols].astype(F32)
        gb = g.astype(BF)
        v = b.vals[:, cols]
        prod = g * b.pure[:, cols]
        outs = []
        for e in (0, 1):
            k = 2 * j + e
            here = low if e == 0 else jnp.logical_not(low)
            x = dot(gb, jnp.where(here, v, 0.0).astype(BF), 1, 1)
            decay = b.decay[k]
            st = step[k: k + 1, :]
            xd = x * decay
            dscore = dscore + xd * st
            sums.append(jnp.sum(xd * scores, axis=0, keepdims=True))
            rowcols = jnp.where(
                at_lane == k, jnp.sum(jnp.where(here, prod, 0.0), axis=1, keepdims=True), rowcols
            )
            wt = (decay * scores * st).T.astype(BF)
            outs.append(dot(wt, gb))
        skips = jnp.where(low, skip[0, head0 + 2 * j], skip[0, head0 + 2 * j + 1])
        b.vghalf[:, cols] = (jnp.where(low, outs[0], outs[1]) + skips * g).astype(BF)
    b.vg.at[rows(y)][:, half(zh)] = b.vghalf[...]
    go(gather_z(b.vg, b.k_sem))
    for rel in arrival(NY):
        go(gather_y(b.vg, b.k_sem, rel))
    dstep = jnp.concatenate(sums, axis=0)
    dcum = rowcols.T[:HH, :] - step * dstep
    ddecay = dot(dcum, causal.astype(F32), precision=HI)
    draw = (dstep - rate * ddecay) * jax.nn.sigmoid(raw)
    drw = jnp.where(low, dot(dscore.T, wr, precision=HI), dot(dscore, wr, precision=HI))
    in_half = lax.broadcasted_iota(jnp.int32, (HB, T), 0) // HH == zh
    dsteps = jnp.where(in_half, jnp.concatenate([draw] * NZ, axis=0), 0.0)

    b.j1send[:T, :] = drw.astype(BF)
    b.j1send[T:, :] = dsteps.astype(BF)
    j1 = go(send(b.j1send, b.j1rec, b.z_sem, 3, zdev))
    j1.wait_recv()
    b.j2send[:T, :] = (drw + b.j1rec[:T, :].astype(F32)).astype(BF)
    b.j2send[T:, :] = (dsteps + b.j1rec[T:, :].astype(F32)).astype(BF)
    b.j2rec.at[d][...] = b.j2send[...]

    def j2_copy(k):
        return send(b.j2send, b.j2rec.at[d], b.j2_sem, k, xdev((d + k) % ND))

    for k in arrival(ND):
        go(j2_copy(k))
    gather_z(b.vg, b.k_sem).wait_recv()
    for rel in arrival(NY):
        go(forward_y(b.vg, b.k_sem, rel))
    for k in arrival(ND):
        j2_copy(k).wait_recv()
    part = b.j2rec[0, :T, :].astype(F32)
    for q in range(1, ND):
        part = part + b.j2rec[q, :T, :].astype(F32)
    b.j3send[:T, :] = part.astype(BF)
    for q in range(ND):
        b.j3send[T + HB * q: T + HB * (q + 1), :] = b.j2rec[q, T:, :]
    b.j3rec.at[y][...] = b.j3send[...]

    def j3_copy(k):
        return send(b.j3send, b.j3rec.at[y], b.j3_sem, k, ydev((y + k) % NY))

    for k in arrival(NY):
        go(j3_copy(k))
    loss_z().wait_recv()
    b.lout[...] = (
        jnp.zeros((8, 128), F32) + jnp.sum(b.lsum[2] + b.lrec[ND + NY]) / (T * ND * F * NY * NZ)
    )
    loss_copy = pltpu.make_async_copy(b.lout, loss, b.store_sem.at[1])
    loss_copy.start()

    for k in arrival(NY):
        gather_y(b.vg, b.k_sem, k).wait_recv()
        forward_y(b.vg, b.k_sem, k).wait_recv()
    in_copies = []
    for n in range(F // 128 // 2 if F >= 256 else 1):
        w = min(256, F)
        b.gin[w * n: w * (n + 1), :] = dot(b.srct[w * n: w * (n + 1), :], b.vg[...]).astype(BF)
        cp = pltpu.make_async_copy(
            b.gin.at[pl.ds(w * n, w)], g_in.at[0, pl.ds(w * n, w)], b.store_sem.at[2 + n]
        )
        cp.start()
        in_copies.append(cp)
    for k in arrival(NY):
        j3_copy(k).wait_recv()
    for q in range(NY):
        b.sg[T * q: T * (q + 1), : 2 * NS] = b.j3rec[q, :T, :]
        b.sg[T * q: T * (q + 1), 2 * NS:] = b.j3rec[q, T:, :].T
    b.gside[...] = dot(b.srct[...], b.sg[...]).astype(BF)
    side_copy = pltpu.make_async_copy(b.gside, g_side.at[0], b.store_sem.at[1 + 1 + cfg.nin])
    side_copy.start()

    for cp in pending:
        cp.wait_send()
    for rel in range(1, NY):
        for cp in c_copies(rel):
            cp.wait_send()
        i_copy(rel).wait_send()
    for rel in range(1, ND):
        f_copy(rel).wait_send()
    out_copy.wait()
    loss_copy.wait()
    side_copy.wait()
    for cp in in_copies:
        cp.wait()


def local(states, final_state, retained, block_slot, w_in, w_side, w_out, a_rate, dt_bias, skip):
    nd, sec, nt = lax.axis_size("dp"), lax.axis_size("section"), lax.axis_size("tensor")
    ny = nt // NZ
    t, f = final_state.shape
    c = w_in.shape[2]
    heads = a_rate.shape[1]
    hb = c // P_SIZE
    side = t + hb
    sd = 2 * NS + heads
    h = c // NZ
    n = t * nd
    nin = max(1, f // 256)
    assert ny == nd and t == 128
    V = pltpu.VMEM

    def sems(k):
        return pltpu.SemaphoreType.DMA((2, k))

    scratch = dict(
        layers=V((2 * sec, t // sec, f), BF), stage=V((2, sec, t // sec, f), BF),
        src=V((n, f), BF), tgt=V((t, f), BF), final=V((t, f), BF), srct=V((f, n), BF),
        win=V((f, c), BF), wside=V((f, sd), BF), wout=V((c, f), BF), wstep=V((hb, f), BF),
        psend=V((ny, t, c), BF), prec=V((ny, t, c), BF),
        ssend=V((ny, side, 128), BF), srec=V((ny, side, 128), BF),
        zsend=V((t, h), BF), zrec=V((t, h), BF), zssend=V((side, 128), BF), zsrec=V((side, 128), BF),
        side=V((side, 128), F32), vals=V((t, h), F32), pure=V((t, h), F32),
        decay=V((hb // NZ, t, t), F32), mhalf=V((t, h), BF), mix=V((n, c), BF), mixt=V((c, n), BF),
        osend=V((nd, t, f), BF), orec=V((nd, t, f), BF), ogown=V((t, f), BF), og=V((n, f), BF),
        lsum=V((3, 8, 128), F32), lrec=V((nd + ny + 1, 8, 128), F32), lout=V((8, 128), F32),
        isend=V((ny, t, c), BF), irec=V((ny, t, c), BF), izsend=V((t, h), BF), izrec=V((t, h), BF),
        gout=V((c, f), BF), vghalf=V((t, h), BF), vg=V((n, c), BF),
        j1send=V((side, 128), BF), j1rec=V((side, 128), BF),
        j2send=V((side, 128), BF), j2rec=V((nd, side, 128), BF),
        j3send=V((t + heads, 128), BF), j3rec=V((ny, t + heads, 128), BF), sg=V((n, sd), BF),
        gin=V((f, c), BF), gside=V((f, sd), BF),
        load_sem=pltpu.SemaphoreType.DMA((5,)), store_sem=pltpu.SemaphoreType.DMA((3 + nin,)),
        h1_sem=sems(sec), h2_sem=sems(sec), h3_sem=sems(sec), ag_sem=sems(nd),
        c_sem=sems(ny), cs_sem=sems(ny), z_sem=sems(4), e_sem=sems(2 * ny), f_sem=sems(nd),
        h_sem=sems(nd), i_sem=sems(ny), l_sem=sems(nd + ny + 1), k_sem=sems(2 * ny),
        j2_sem=sems(nd), j3_sem=sems(ny),
    )
    cfg = SimpleNamespace(
        names=tuple(scratch), nd=nd, sec=sec, ny=ny, t=t, f=f, c=c, hb=hb, heads=heads, nin=nin
    )
    hbm = pl.BlockSpec(memory_space=pl.ANY)
    smem = pl.BlockSpec(memory_space=pltpu.SMEM)
    g_in, g_side, g_out, loss = pl.pallas_call(
        functools.partial(kernel, cfg, None),
        out_shape=(
            jax.ShapeDtypeStruct(w_in.shape, BF), jax.ShapeDtypeStruct(w_side.shape, BF),
            jax.ShapeDtypeStruct(w_out.shape, BF), jax.ShapeDtypeStruct((8, 128), F32),
        ),
        in_specs=[hbm, hbm, smem, smem, hbm, hbm, hbm, smem, smem, smem],
        out_specs=(hbm, hbm, hbm, hbm),
        scratch_shapes=list(scratch.values()),
        compiler_params=pltpu.CompilerParams(
            collective_id=0, has_side_effects=True, vmem_limit_bytes=48 << 20
        ),
        name="distill",
    )(states, final_state, retained, block_slot, w_in, w_side, w_out, a_rate, dt_bias, skip)
    return g_in, g_side, g_out, loss[0, :1]


def solution(mesh):
    placed = (
        P("section", "dp", "tensor"),
        P("dp", "tensor"),
        P(),
        P(),
        P("section", "tensor", "dp"),
        P("section", "tensor", None),
        P("section", "dp", "tensor"),
        P("section", None),
        P("section", None),
        P("section", None),
    )
    return jax.shard_map(
        local,
        mesh=mesh,
        in_specs=placed,
        out_specs=(
            P("section", "tensor", "dp"),
            P("section", "tensor", None),
            P("section", "dp", "tensor"),
            P("section"),
        ),
        check_vma=False,
    )
```

time: 845 us -> 170 us (0.20)
  the two profiles are of different devices: /device:TPU:32 before, /device:TPU:16 now
where the time goes in v1:
time: 170 us
  Pallas kernels  155 us (91%)
  local copies, waits for them, and re-layouts  13.6 us (8%)
    pallas_call x1, Pallas kernels, local(): pl.pallas_call(functools.partial(kernel, cfg, None), out_shape=(jax.Shape...  155 us
    unnamed x20, local copies, waits for them, and re-layouts  13.1 us

profile of v1, /device:TPU:16, one launch (start us, length us, event | category | flops | bytes accessed | tf_op | source)
XLA Modules:
  0.0 169.7 jit_solution(8955172597130270741)
XLA Ops:
  0.6 1.2 copy.14.w_side
  1.8 0.0 copy-start.1
  1.8 1.0 copy-done.1
  2.9 0.0 copy-start.2
  2.9 0.9 copy-done.2
  3.8 0.0 copy-start.3
  3.8 0.7 copy-done.3
  4.5 0.0 copy-start.4
  4.5 0.7 copy-done.4
  5.1 0.0 copy-start.5
  5.1 0.7 copy-done.5
  5.8 0.0 copy-start.6
  5.8 0.7 copy-done.6
  6.5 0.0 copy-start.7
  6.5 0.7 copy-done.7
  7.1 155.4 %distill.1 = (bf16[1,1024,1024]{2,1,0:T(8,128)(2,1)S(1)}, bf16[1,1024,192]{2,1,0:T(8,128)(2,1)S(1)}, bf16[1,1024,1024]{2,1,0:T(8,128)(2,1)S(1)}, f32[8,128]{1,0:T(8,128)S(1)}) custom-call(bf16[2,128,1024]{2,1,0:T(8,128)(2,1)S(1)} %copy-done.1, bf16[128,1024]{1,0:T(8,128)(2,1)S(1)} %copy-done.2, s32[8]{0:T(128)S(1)} %copy-done.3, s32[8]{0:T(128)S(1)} %copy-done.4, ...), custom_call_target="tpu_custom_call" | custom-call | tf_op jit(solution)/shard_map/distill/pallas_call | solution.py:530
  162.6 0.0 copy-start
  162.6 1.3 copy-done
  163.9 0.5 slice.3
  164.4 0.9 copy.15
  165.3 3.1 %copy.18 = bf16[1,1024,1024]{2,1,0:T(8,128)(2,1)} copy(bf16[1,1024,1024]{2,1,0:T(8,128)(2,1)} %copy-done) | data formatting | bytes 4194304
  168.4 1.3 copy.19
Async XLA Ops:
  1.8 1.0 copy-start.1
  2.9 0.9 copy-start.2
  3.8 0.7 copy-start.3
  4.5 0.7 copy-start.4
  5.1 0.7 copy-start.5
  5.8 0.7 copy-start.6
  6.5 0.7 copy-start.7
  162.6 1.3 copy-start

commit v2 on v1

v2 whole, which is shorter than its diff:
```python
import functools
from types import SimpleNamespace

import jax
import jax.numpy as jnp
from jax import lax
from jax.experimental import pallas as pl
from jax.experimental.pallas import tpu as pltpu
from jax.sharding import PartitionSpec as P

P_SIZE = 64
NS = 64
NZ = 2
MESH = pl.DeviceIdType.MESH
F32 = jnp.float32
BF = jnp.bfloat16
HI = lax.Precision.HIGHEST


def dot(a, b, ca=1, cb=0, precision=None):
    return lax.dot_general(
        a, b, (((ca,), (cb,)), ((), ())), preferred_element_type=F32, precision=precision
    )


class Copy:
    def __init__(self, copy, key, due):
        self.copy, self.key, self.due = copy, key, due
        self.start, self.wait_send = copy.start, copy.wait_send

    def wait_recv(self):
        self.copy.wait_recv()
        self.due.pop(self.key, None)


def arrival(n):
    return sorted(range(1, n), key=lambda k: min(k, n - k))


def kernel(cfg, stop, states, final, retained, slot, w_in, w_side, w_out, a_rate, dt_bias, skip,
           g_in, g_side, g_out, loss, *scratch):
    b = SimpleNamespace(**dict(zip(cfg.names, scratch)))
    ND, SEC, NY = cfg.nd, cfg.sec, cfg.ny
    T, F, C, H = cfg.t, cfg.f, cfg.c, cfg.c // NZ
    HB, HH = cfg.hb, cfg.hb // NZ
    NC = SEC // 2
    RC, CR = T // SEC, T // NC
    W = 2 * NS
    d, s, t = lax.axis_index("dp"), lax.axis_index("section"), lax.axis_index("tensor")
    zh, y = t // NY, t % NY
    oz = 1 - zh
    zl, core = s // 2, s % 2

    def xdev(i):
        return (i, s, t)

    def ydev(i):
        return (d, s, zh * NY + i)

    zdev = (d, s, oz * NY + y)

    if NC == 4:
        chips = [zl, zl + 1 - 2 * (zl % 2), (zl + 2) % 4, 3 - zl]
    else:
        chips = [zl, 1 - zl]
    sections = [2 * c + k for c in chips for k in (core, 1 - core)]
    far_first = [m for i in (2, 3, 1, 0) for m in (2 * i, 2 * i + 1) if 0 < m < SEC]

    def sdev(m):
        return (d, sections[m], t)

    bar = pltpu.get_barrier_semaphore()
    partners = (
        [sdev(m) for m in far_first]
        + [xdev((d + k) % ND) for k in range(1, ND)]
        + [ydev((y + k) % NY) for k in range(1, NY)]
        + [zdev]
    )
    for p in partners:
        pl.semaphore_signal(bar, inc=1, device_id=p, device_id_type=MESH)

    def rows(i, n):
        return pl.ds(pl.multiple_of(i * n, 16), n)

    def half(i):
        return pl.ds(pl.multiple_of(i * H, 128), H)

    loads = [
        pltpu.make_async_copy(src, dst, b.load_sem.at[i])
        for i, (src, dst) in enumerate((
            (states.at[:, rows(s, RC)], b.layers.at[pl.ds(2 * s, 2)]),
            (retained, b.retained), (slot, b.slot), (w_side.at[0], b.wside), (w_in.at[0], b.win),
            (a_rate, b.rate), (dt_bias, b.bias), (skip, b.skip), (w_out.at[0], b.wout), (final, b.final),
        ))
    ]
    for cp in loads:
        cp.start()
    loading = dict(enumerate(loads))

    def loaded(*which):
        for i in which:
            loading.pop(i).wait()

    def send(src, dst, sems, i, dev):
        cp = pltpu.make_async_remote_copy(
            src_ref=src, dst_ref=dst, send_sem=sems.at[0, i], recv_sem=sems.at[1, i],
            device_id=dev, device_id_type=MESH,
        )
        return Copy(cp, (id(sems), i), due)

    pending, due = [], {}

    def go(cp):
        cp.start()
        pending.append(cp)
        due[cp.key] = cp
        return cp

    def finish():
        for cp in list(due.values()):
            cp.wait_recv()
        for i in list(loading):
            loaded(i)
        for cp in pending:
            cp.wait_send()

    pl.semaphore_wait(bar, len(partners))

    hop1 = [
        go(send(states.at[:, rows(sections[m], RC)], b.layers.at[pl.ds(2 * s, 2)], b.h1_sem, m, sdev(m)))
        for m in far_first
    ]
    loaded(0, 1, 2, 3)
    wanted = []
    for i in range(SEC):
        layer = jnp.int32(0)
        for r in range(SEC):
            layer = layer + jnp.where(b.slot[r] == i, b.retained[r], 0)
        wanted.append(layer)

    def wanted_of(i):
        out = jnp.int32(0)
        for j in range(SEC):
            out = out + jnp.where(i == j, wanted[j], 0)
        return out

    layer_of = [wanted_of(i) for i in sections]
    pick = (
        lax.broadcasted_iota(jnp.int32, (HB, cfg.heads), 1)
        == lax.broadcasted_iota(jnp.int32, (HB, cfg.heads), 0) + d * HB
    )
    b.wstep[...] = dot(pick.astype(BF), b.wside[W:, :]).astype(BF)

    for cp in hop1:
        cp.wait_recv()
    mine = rows(core, RC)
    b.src[zl, d, mine, :] = b.layers[layer_of[0]]
    hop2 = {}
    for m in range(1, SEC):
        b.stage[0, m] = b.layers[layer_of[m]]
        hop2[m] = go(send(b.stage.at[0, m], b.src.at[zl, d, mine], b.h2_sem, m, sdev(m)))

    def g_copy(i, k):
        at = b.src.at[chips[i], d]
        return send(at, at, b.g_sem, i * ND + k, xdev((d + k) % ND))

    for i in range(NC):
        for m in (2 * i, 2 * i + 1):
            if m:
                hop2[m].wait_recv()
        for k in arrival(ND):
            go(g_copy(i, k))
    hop3 = []
    for m in range(1, SEC):
        b.stage[1, m] = b.layers[jnp.minimum(layer_of[m] + 1, 2 * SEC - 1)]
        hop3.append(go(send(b.stage.at[1, m], b.tgt.at[rows(s, RC)], b.h3_sem, m, sdev(m))))
    b.tgt[rows(s, RC), :] = b.layers[jnp.minimum(layer_of[0] + 1, 2 * SEC - 1)]
    loaded(4)

    NB = 256

    def product(lhs, c, w, out, i, transposed=False):
        def step(n, carry):
            cols = pl.ds(pl.multiple_of(n * NB, NB), NB)
            w_n = w[cols, :] if transposed else w[:, cols]
            x = lhs[c].reshape(ND * CR, lhs.shape[3])
            r = dot(x, w_n, 1, 1 if transposed else 0).astype(BF)
            out[i, :, :, cols] = r.reshape(ND, CR, NB)
            return carry

        lax.fori_loop(0, (w.shape[0] if transposed else w.shape[1]) // NB, step, 0)

    def c_copy(i, rel):
        q = (y + rel) % NY
        return send(b.psend.at[i, q], b.prec.at[i, rel], b.c_sem, i * NY + rel, ydev(q))

    def z_copy(i):
        return send(b.zsend.at[i], b.zrec.at[i], b.z_sem, i, zdev)

    def c_step(i):
        for k in arrival(ND):
            g_copy(i, k).wait_recv()
        c = chips[i]
        product(b.src, c, b.win, b.psend, i)
        x = b.src[c].reshape(ND * CR, F)
        b.psend[i, :, :, C:] = dot(x, b.wside[:W, :], 1, 1).astype(BF).reshape(ND, CR, W)
        for rel in arrival(NY):
            go(c_copy(i, rel))

    def c_sum(i):
        for rel in range(1, NY):
            c_copy(i, rel).wait_recv()

        def total(cols):
            out = b.psend[i, y, :, cols].astype(F32)
            for rel in range(1, NY):
                out = out + b.prec[i, rel, :, cols].astype(F32)
            return out

        b.zsend[i, :, :H] = total(half(oz)).astype(BF)
        side = total(slice(C, C + W))
        b.zsend[i, :, H:] = side.astype(BF)
        go(z_copy(i))
        here = rows(chips[i], CR)
        b.vals[here, :] = total(half(zh))
        b.rw[here, :] = side

    def st_copy(rel):
        return send(b.stsend.at[rel], b.strec.at[rel], b.st_sem, rel, ydev((y + rel) % NY))

    for i in range(NC):
        c_step(i)
        if i:
            c_sum(i - 1)
    for rel in arrival(NY) + [0]:
        x = b.src[:, (y + rel) % NY].reshape(T, F)
        b.stsend[rel] = dot(b.wstep[...], x, 1, 1).astype(BF)
        if rel:
            go(st_copy(rel))
    for c in range(NC):
        for j in range(F // 128):
            b.srct[128 * j: 128 * (j + 1), ND * CR * c: ND * CR * (c + 1)] = (
                b.src[c, :, :, 128 * j: 128 * (j + 1)].reshape(ND * CR, 128).T
            )
    c_sum(NC - 1)
    steps = b.stsend[0].astype(F32)
    for rel in range(1, NY):
        st_copy(rel).wait_recv()
        steps = steps + b.strec[rel].astype(F32)
    b.stz[0] = steps.astype(BF)
    stz = go(send(b.stz.at[0], b.stz.at[1], b.st_sem, NY, zdev))
    loaded(5, 6, 7)
    for i in range(NC):
        z_copy(i).wait_recv()
        here = rows(chips[i], CR)
        b.vals[here, :] += b.zrec[i, :, :H].astype(F32)
        b.rw[here, :] += b.zrec[i, :, H:].astype(F32)
    stz.wait_recv()
    b.steps[...] = steps + b.stz[1].astype(F32)

    head0 = d * HB + zh * HH

    def column(ref):
        at = lax.broadcasted_iota(jnp.int32, (HH, 1), 0)
        out = jnp.zeros((HH, 1), F32)
        for k in range(HH):
            out = jnp.where(at == k, ref[0, head0 + k], out)
        return out

    rate, bias = column(b.rate), column(b.bias)
    r_t = lax.broadcasted_iota(jnp.int32, (T, T), 0)
    r_u = lax.broadcasted_iota(jnp.int32, (T, T), 1)
    causal = r_t >= r_u
    low = r_u < NS
    raw = b.steps[pl.ds(pl.multiple_of(zh * HH, 8), HH), :] + bias
    step = jax.nn.softplus(raw)
    cum = dot(-(step * rate), (r_t <= r_u).astype(F32), precision=HI)
    rw = b.rw[...]
    wr = pltpu.roll(rw, NS, 1)
    scores = dot(jnp.where(low, wr, 0.0), rw, 1, 1, precision=HI)
    cum_cols = jnp.concatenate([cum] * (T // HH), axis=0).T
    for k in range(HH):
        diff = cum_cols[:, k: k + 1] - cum[k: k + 1, :]
        b.decay[k] = jnp.where(causal, jnp.exp(jnp.where(causal, diff, 0.0)), 0.0)

    def lanes(j):
        return pl.ds(pl.multiple_of(zh * H + 128 * j, 128), 128)

    for j in range(H // 128):
        cols = slice(128 * j, 128 * (j + 1))
        v = b.vals[:, cols]
        vb = v.astype(BF)
        outs = []
        for k in (2 * j, 2 * j + 1):
            w = (b.decay[k] * scores * step[k: k + 1, :]).astype(BF)
            outs.append(dot(w, vb))
        y2 = jnp.where(low, outs[0], outs[1])
        b.pure[:, cols] = y2
        skips = jnp.where(low, b.skip[0, head0 + 2 * j], b.skip[0, head0 + 2 * j + 1])
        b.mix[:, y, :, lanes(j)] = (y2 + skips * v).astype(BF).reshape(NC, CR, 128)

    def spread_z(buf, sems, c):
        at = buf.at[c, y, :, half(zh)]
        return send(at, at, sems, c, zdev)

    def spread_y(buf, sems, c, rel, which):
        at = buf.at[c, y, :, half(oz if which else zh)]
        return send(at, at, sems, NC + (2 * c + which) * NY + rel, ydev((y + rel) % NY))

    def spread(buf, sems):
        for c in range(NC):
            go(spread_z(buf, sems, c))
            for rel in arrival(NY):
                go(spread_y(buf, sems, c, rel, 0))

    def spread_on(buf, sems):
        for c in range(NC):
            spread_z(buf, sems, c).wait_recv()
            for rel in arrival(NY):
                go(spread_y(buf, sems, c, rel, 1))

    def spread_done(buf, sems, c):
        for rel in arrival(NY):
            for which in (0, 1):
                spread_y(buf, sems, c, rel, which).wait_recv()

    spread(b.mix, b.e_sem)
    loaded(8)
    spread_on(b.mix, b.e_sem)

    def f_copy(c, rel):
        q = (d + rel) % ND
        return send(b.osend.at[c, q], b.orec.at[c, rel], b.f_sem, c * ND + rel, xdev(q))

    for c in range(NC):
        spread_done(b.mix, b.e_sem, c)
        product(b.mix, c, b.wout, b.osend, c)
        for rel in arrival(ND):
            go(f_copy(c, rel))
    for c in range(NC):
        for j in range(C // 128):
            b.mixt[128 * j: 128 * (j + 1), NY * CR * c: NY * CR * (c + 1)] = (
                b.mix[c, :, :, 128 * j: 128 * (j + 1)].reshape(NY * CR, 128).T
            )
    loaded(9)
    for cp in hop3:
        cp.wait_recv()
    inner = layer_of[0] + 1 < 2 * SEC

    def h_copy(c, k):
        at = b.og.at[c, d]
        return send(at, at, b.h_sem, c * ND + k, xdev((d + k) % ND))

    total = jnp.zeros((8, 128), F32)
    for c in range(NC):
        for rel in range(1, ND):
            f_copy(c, rel).wait_recv()
        for j in range(F // 128):
            cols = slice(128 * j, 128 * (j + 1))
            here = slice(CR * c, CR * (c + 1))
            out = b.osend[c, d, :, cols].astype(F32)
            for rel in range(1, ND):
                out = out + b.orec[c, rel, :, cols].astype(F32)
            goal = jnp.where(inner, b.tgt[here, cols].astype(F32), b.final[here, cols].astype(F32))
            err = out - goal
            b.og[c, d, :, cols] = (2.0 * err / (T * ND)).astype(BF)
            total = total + jnp.sum((err * err).reshape(CR // 8, 8, 128), axis=0)
        for k in arrival(ND):
            go(h_copy(c, k))
    b.lsum[0] = total

    def loss_x(k):
        return send(b.lsum.at[0], b.lrec.at[k], b.l_sem, k, xdev((d + k) % ND))

    def loss_y(k):
        return send(b.lsum.at[1], b.lrec.at[ND + k], b.l_sem, ND + k, ydev((y + k) % NY))

    def loss_z():
        return send(b.lsum.at[2], b.lrec.at[ND + NY], b.l_sem, ND + NY, zdev)

    for k in range(1, ND):
        go(loss_x(k))

    def i_copy(c, rel):
        q = (y + rel) % NY
        return send(b.isend.at[c, q], b.irec.at[c, rel], b.i_sem, c * NY + rel, ydev(q))

    def iz_copy(c):
        return send(b.izsend.at[c], b.izrec.at[c], b.iz_sem, c, zdev)

    def i_step(c):
        for k in arrival(ND):
            h_copy(c, k).wait_recv()
        product(b.og, c, b.wout, b.isend, c, transposed=True)
        for rel in arrival(NY):
            go(i_copy(c, rel))

    def i_sum(c):
        for rel in range(1, NY):
            i_copy(c, rel).wait_recv()

        def total(cols):
            out = b.isend[c, y, :, cols].astype(F32)
            for rel in range(1, NY):
                out = out + b.irec[c, rel, :, cols].astype(F32)
            return out

        b.izsend[c] = total(half(oz)).astype(BF)
        go(iz_copy(c))
        b.grad[CR * c: CR * (c + 1), :] = total(half(zh))

    for c in range(NC):
        i_step(c)
        if c:
            i_sum(c - 1)
    total = b.lsum[0]
    for k in range(1, ND):
        loss_x(k).wait_recv()
        total = total + b.lrec[k]
    b.lsum[1] = total
    for k in range(1, NY):
        go(loss_y(k))
    i_sum(NC - 1)

    def store(n, carry):
        at = pl.ds(pl.multiple_of(n * 256, 256), 256)
        b.gout[at, :] = dot(b.mixt[at, :], b.og[...].reshape(ND * T, F)).astype(BF)
        return carry

    lax.fori_loop(0, C // 256, store, 0)
    total = b.lsum[1]
    for k in range(1, NY):
        loss_y(k).wait_recv()
        total = total + b.lrec[ND + k]
    b.lsum[2] = total
    go(loss_z())
    for c in range(NC):
        iz_copy(c).wait_recv()
        b.grad[CR * c: CR * (c + 1), :] += b.izrec[c].astype(F32)

    dscore = jnp.zeros((T, T), F32)
    sums = []
    at_lane = lax.broadcasted_iota(jnp.int32, (T, 128), 1)
    rowcols = jnp.zeros((T, 128), F32)
    for j in range(H // 128):
        cols = slice(128 * j, 128 * (j + 1))
        g = b.grad[:, cols]
        gb = g.astype(BF)
        v = b.vals[:, cols]
        prod = g * b.pure[:, cols]
        outs = []
        for e in (0, 1):
            k = 2 * j + e
            here = low if e == 0 else jnp.logical_not(low)
            x = dot(gb, jnp.where(here, v, 0.0).astype(BF), 1, 1)
            decay = b.decay[k]
            st = step[k: k + 1, :]
            xd = x * decay
            dscore = dscore + xd * st
            sums.append(jnp.sum(xd * scores, axis=0, keepdims=True))
            rowcols = jnp.where(
                at_lane == k, jnp.sum(jnp.where(here, prod, 0.0), axis=1, keepdims=True), rowcols
            )
            wt = (decay * scores * st).T.astype(BF)
            outs.append(dot(wt, gb))
        skips = jnp.where(low, b.skip[0, head0 + 2 * j], b.skip[0, head0 + 2 * j + 1])
        b.vg[:, y, :, lanes(j)] = (
            (jnp.where(low, outs[0], outs[1]) + skips * g).astype(BF).reshape(NC, CR, 128)
        )
    for c in range(NC):
        for rel in arrival(NY):
            go(spread_y(b.vg, b.k_sem, c, rel, 0))
    dstep = jnp.concatenate(sums, axis=0)
    dcum = rowcols.T[:HH, :] - step * dstep
    ddecay = dot(dcum, causal.astype(F32), precision=HI)
    draw = (dstep - rate * ddecay) * jax.nn.sigmoid(raw)
    drw = jnp.where(low, dot(dscore.T, wr, precision=HI), dot(dscore, wr, precision=HI)).T
    in_half = lax.broadcasted_iota(jnp.int32, (HB, T), 0) // HH == zh
    dsteps = jnp.where(in_half, jnp.concatenate([draw] * NZ, axis=0), 0.0)

    b.j1send[:W, :] = drw.astype(BF)
    b.j1send[W:, :] = dsteps.astype(BF)
    j1 = go(send(b.j1send, b.j1rec, b.iz_sem, NC, zdev))
    for c in range(NC):
        go(spread_z(b.vg, b.k_sem, c))
    j1.wait_recv()
    b.j2send[:W, :] = (drw + b.j1rec[:W, :].astype(F32)).astype(BF)
    b.j2send[W:, :] = (dsteps + b.j1rec[W:, :].astype(F32)).astype(BF)
    b.j2rec[d] = b.j2send[...]

    def j2_copy(k):
        return send(b.j2send, b.j2rec.at[d], b.j2_sem, k, xdev((d + k) % ND))

    for k in arrival(ND):
        go(j2_copy(k))
    spread_on(b.vg, b.k_sem)
    for k in arrival(ND):
        j2_copy(k).wait_recv()
    part = b.j2rec[0, :W, :].astype(F32)
    for q in range(1, ND):
        part = part + b.j2rec[q, :W, :].astype(F32)
    b.j3[y, :W, :] = part.astype(BF)
    for q in range(ND):
        b.j3[y, W + HB * q: W + HB * (q + 1), :] = b.j2rec[q, W:, :]

    def j3_copy(k):
        return send(b.j3.at[y], b.j3.at[y], b.j3_sem, k, ydev((y + k) % NY))

    for k in arrival(NY):
        go(j3_copy(k))
    loss_z().wait_recv()
    b.lout[...] = (
        jnp.zeros((8, 128), F32) + jnp.sum(b.lsum[2] + b.lrec[ND + NY]) / (T * ND * F * NY * NZ)
    )
    stores = []

    def write(src, dst):
        cp = pltpu.make_async_copy(src, dst, b.store_sem.at[len(stores)])
        cp.start()
        stores.append(cp)

    write(b.lout, loss)
    write(b.gout, g_out.at[0])
    for c in range(NC):
        spread_done(b.vg, b.k_sem, c)
    w = min(256, F)
    for n in range(F // w):
        b.gin[w * n: w * (n + 1), :] = dot(
            b.srct[w * n: w * (n + 1), :], b.vg[...].reshape(ND * T, C)
        ).astype(BF)
        write(b.gin.at[pl.ds(w * n, w)], g_in.at[0, pl.ds(w * n, w)])
    for k in arrival(NY):
        j3_copy(k).wait_recv()
    out = jnp.zeros((W + cfg.heads, F), F32)
    for q in range(NY):
        out = out + dot(b.j3[q], b.src[:, q].reshape(T, F))
    b.gside[...] = out.astype(BF)
    write(b.gside, g_side.at[0])

    finish()
    for cp in stores:
        cp.wait()


def local(states, final_state, retained, block_slot, w_in, w_side, w_out, a_rate, dt_bias, skip):
    nd, sec, nt = lax.axis_size("dp"), lax.axis_size("section"), lax.axis_size("tensor")
    ny = nt // NZ
    t, f = final_state.shape
    c = w_in.shape[2]
    heads = a_rate.shape[1]
    hb = c // P_SIZE
    sd = 2 * NS + heads
    side = 2 * NS + hb
    h = c // NZ
    n = t * nd
    nc = sec // 2
    cr = t // nc
    nstore = 3 + max(1, f // 256)
    assert ny == nd and t == 128
    V, S = pltpu.VMEM, pltpu.SMEM

    def sems(k):
        return pltpu.SemaphoreType.DMA((2, k))

    scratch = dict(
        retained=S((sec,), jnp.int32), slot=S((sec,), jnp.int32),
        rate=S((1, heads), F32), bias=S((1, heads), F32), skip=S((1, heads), F32),
        layers=V((2 * sec, t // sec, f), BF), stage=V((2, sec, t // sec, f), BF),
        src=V((nc, nd, cr, f), BF), tgt=V((t, f), BF), final=V((t, f), BF), srct=V((f, n), BF),
        win=V((f, c), BF), wside=V((sd, f), BF), wout=V((c, f), BF), wstep=V((hb, f), BF),
        psend=V((nc, ny, cr, c + 2 * NS), BF), prec=V((nc, ny, cr, c + 2 * NS), BF),
        zsend=V((nc, cr, h + 2 * NS), BF), zrec=V((nc, cr, h + 2 * NS), BF),
        stsend=V((ny, hb, t), BF), strec=V((ny, hb, t), BF), stz=V((2, hb, t), BF),
        steps=V((hb, t), F32), rw=V((t, 2 * NS), F32), vals=V((t, h), F32), pure=V((t, h), F32),
        decay=V((hb // NZ, t, t), F32), mix=V((nc, ny, cr, c), BF), mixt=V((c, n), BF),
        osend=V((nc, nd, cr, f), BF), orec=V((nc, nd, cr, f), BF), og=V((nc, nd, cr, f), BF),
        lsum=V((3, 8, 128), F32), lrec=V((nd + ny + 1, 8, 128), F32), lout=V((8, 128), F32),
        isend=V((nc, ny, cr, c), BF), irec=V((nc, ny, cr, c), BF),
        izsend=V((nc, cr, h), BF), izrec=V((nc, cr, h), BF), grad=V((t, h), F32),
        gout=V((c, f), BF), vg=V((nc, ny, cr, c), BF),
        j1send=V((side, t), BF), j1rec=V((side, t), BF),
        j2send=V((side, t), BF), j2rec=V((nd, side, t), BF), j3=V((ny, sd, t), BF),
        gin=V((f, c), BF), gside=V((sd, f), BF),
        load_sem=pltpu.SemaphoreType.DMA((10,)), store_sem=pltpu.SemaphoreType.DMA((nstore,)),
        h1_sem=sems(sec), h2_sem=sems(sec), h3_sem=sems(sec), g_sem=sems(nc * nd),
        c_sem=sems(nc * ny), z_sem=sems(nc), st_sem=sems(ny + 1), e_sem=sems(nc + 2 * nc * ny),
        f_sem=sems(nc * nd), h_sem=sems(nc * nd), i_sem=sems(nc * ny), iz_sem=sems(nc + 1),
        l_sem=sems(nd + ny + 1), k_sem=sems(nc + 2 * nc * ny), j2_sem=sems(nd), j3_sem=sems(ny),
    )
    cfg = SimpleNamespace(
        names=tuple(scratch), nd=nd, sec=sec, ny=ny, t=t, f=f, c=c, hb=hb, heads=heads
    )
    hbm = pl.BlockSpec(memory_space=pltpu.HBM)
    anywhere = pl.BlockSpec(memory_space=pl.ANY)
    g_in, g_side, g_out, loss = pl.pallas_call(
        functools.partial(kernel, cfg, None),
        out_shape=(
            jax.ShapeDtypeStruct(w_in.shape, BF), jax.ShapeDtypeStruct((1, sd, f), BF),
            jax.ShapeDtypeStruct(w_out.shape, BF), jax.ShapeDtypeStruct((8, 128), F32),
        ),
        in_specs=[hbm] * 10,
        out_specs=(anywhere,) * 4,
        scratch_shapes=list(scratch.values()),
        compiler_params=pltpu.CompilerParams(
            collective_id=0, has_side_effects=True, vmem_limit_bytes=36 << 20
        ),
        name="distill",
    )(
        states, final_state, retained, block_slot, w_in, jnp.swapaxes(w_side, 1, 2), w_out,
        a_rate, dt_bias, skip,
    )
    return g_in, jnp.swapaxes(g_side, 1, 2), g_out, loss[0, :1]


def solution(mesh):
    placed = (
        P("section", "dp", "tensor"),
        P("dp", "tensor"),
        P(),
        P(),
        P("section", "tensor", "dp"),
        P("section", "tensor", None),
        P("section", "dp", "tensor"),
        P("section", None),
        P("section", None),
        P("section", None),
    )
    return jax.shard_map(
        local,
        mesh=mesh,
        in_specs=placed,
        out_specs=(
            P("section", "tensor", "dp"),
            P("section", "tensor", None),
            P("section", "dp", "tensor"),
            P("section"),
        ),
        check_vma=False,
    )
```

time: 170 us -> 137 us (0.81)
  the two profiles are of different devices: /device:TPU:16 before, /device:TPU:32 now
where the time goes in v2:
time: 137 us; the launch traced here: 135 us
  Pallas kernels  121 us (88%)
  local copies, waits for them, and re-layouts  13.3 us (10%)
    pallas_call x1, Pallas kernels, local(): pl.pallas_call(functools.partial(kernel, cfg, None), out_shape=(jax.Shape...  121 us
    unnamed x23, local copies, waits for them, and re-layouts  12.8 us

profile of v2, /device:TPU:32, one launch (start us, length us, event | category | flops | bytes accessed | tf_op | source)
XLA Modules:
  0.0 135.1 jit_solution(255228889919165364)
XLA Ops:
  0.6 0.0 copy-start
  0.6 1.6 %copy-done = bf16[1,1024,1024]{2,1,0:T(8,128)(2,1)S(1)} copy-done((bf16[1,1024,1024]{2,1,0:T(8,128)(2,1)S(1)}, bf16[1,1024,1024]{2,1,0:T(8,128)(2,1)}, u32[]{:S(2)}) %copy-start) | copy-done | bytes 2097176
  2.2 0.0 copy-start.1
  2.2 1.6 %copy-done.1 = bf16[1,1024,1024]{2,1,0:T(8,128)(2,1)S(1)} copy-done((bf16[1,1024,1024]{2,1,0:T(8,128)(2,1)S(1)}, bf16[1,1024,1024]{2,1,0:T(8,128)(2,1)}, u32[]{:S(2)}) %copy-start.1) | copy-done | bytes 2097176
  3.8 0.0 copy-start.2
  3.8 1.0 copy-done.2
  4.9 0.0 copy-start.3
  4.9 1.0 copy-done.3
  5.9 0.0 copy-start.4
  5.9 0.9 copy-done.4
  6.8 0.0 copy-start.5
  6.8 0.7 copy-done.5
  7.5 0.0 copy-start.6
  7.5 0.7 copy-done.6
  8.1 0.0 copy-start.7
  8.1 0.7 copy-done.7
  8.8 0.0 copy-start.8
  8.8 0.7 copy-done.8
  9.4 0.0 copy-start.9
  9.4 0.7 copy-done.9
  10.1 121.1 %distill.1 = (bf16[1,1024,1024]{2,1,0:T(8,128)(2,1)S(1)}, bf16[1,192,1024]{2,1,0:T(8,128)(2,1)S(1)}, bf16[1,1024,1024]{2,1,0:T(8,128)(2,1)S(1)}, f32[8,128]{1,0:T(8,128)S(1)}) custom-call(bf16[2,128,1024]{2,1,0:T(8,128)(2,1)S(1)} %copy-done.2, bf16[128,1024]{1,0:T(8,128)(2,1)S(1)} %copy-done.4, s32[8]{0:T(128)S(1)} %copy-done.5, s32[8]{0:T(128)S(1)} %copy-done.6, ...), custom_call_target="tpu_custom_call" | custom-call | tf_op jit(solution)/shard_map/distill/pallas_call | solution.py:595
  131.2 0.5 slice.3
  131.7 1.3 copy.17
  133.0 0.7 copy.18
  133.8 1.3 copy.19
Async XLA Ops:
  0.6 1.6 %copy-start = (bf16[1,1024,1024]{2,1,0:T(8,128)(2,1)S(1)}, bf16[1,1024,1024]{2,1,0:T(8,128)(2,1)}, u32[]{:S(2)}) copy-start(bf16[1,1024,1024]{2,1,0:T(8,128)(2,1)} %w_in.1) | copy-start | bytes 6291460
  2.2 1.6 %copy-start.1 = (bf16[1,1024,1024]{2,1,0:T(8,128)(2,1)S(1)}, bf16[1,1024,1024]{2,1,0:T(8,128)(2,1)}, u32[]{:S(2)}) copy-start(bf16[1,1024,1024]{2,1,0:T(8,128)(2,1)} %w_out.1) | copy-start | bytes 6291460
  3.8 1.0 copy-start.2
  4.9 1.0 copy-start.3
  5.9 0.9 copy-start.4
  6.8 0.7 copy-start.5
  7.5 0.7 copy-start.6
  8.1 0.7 copy-start.7
  8.8 0.7 copy-start.8
  9.4 0.7 copy-start.9

commit v3 on v2

--- a/solution.py
+++ b/solution.py
@@ -10,6 +10,7 @@
 
 P_SIZE = 64
 NS = 64
+VMEM_BYTES = 60 << 20
 NZ = 2
 MESH = pl.DeviceIdType.MESH
 F32 = jnp.float32
@@ -38,7 +39,7 @@
 
 
 def kernel(cfg, stop, states, final, retained, slot, w_in, w_side, w_out, a_rate, dt_bias, skip,
-           g_in, g_side, g_out, loss, *scratch):
+           srct, vg, g_side, g_out, loss, *scratch):
     b = SimpleNamespace(**dict(zip(cfg.names, scratch)))
     ND, SEC, NY = cfg.nd, cfg.sec, cfg.ny
     T, F, C, H = cfg.t, cfg.f, cfg.c, cfg.c // NZ
@@ -85,11 +86,18 @@
     def half(i):
         return pl.ds(pl.multiple_of(i * H, 128), H)
 
+    PIECES = 2
+    layers = (b.layers0, b.layers1)
+
+    def piece(j):
+        return pl.ds(j * (F // PIECES), F // PIECES)
+
     loads = [
         pltpu.make_async_copy(src, dst, b.load_sem.at[i])
         for i, (src, dst) in enumerate((
-            (states.at[:, rows(s, RC)], b.layers.at[pl.ds(2 * s, 2)]),
-            (retained, b.retained), (slot, b.slot), (w_side.at[0], b.wside), (w_in.at[0], b.win),
+            (states.at[:, rows(s, RC), piece(0)], b.layers0.at[pl.ds(2 * s, 2)]),
+            (states.at[:, rows(s, RC), piece(1)], b.layers1.at[pl.ds(2 * s, 2)]),
+            (retained, b.retained), (slot, b.slot), (w_side.at[0], b.wside), (w_in.at[0], b.win.at[:, pl.ds(0, C)]),
             (a_rate, b.rate), (dt_bias, b.bias), (skip, b.skip), (w_out.at[0], b.wout), (final, b.final),
         ))
     ]
@@ -108,7 +116,12 @@
         )
         return Copy(cp, (id(sems), i), due)
 
-    pending, due = [], {}
+    pending, due, stores = [], {}, []
+
+    def write(src, dst):
+        cp = pltpu.make_async_copy(src, dst, b.store_sem.at[len(stores)])
+        cp.start()
+        stores.append(cp)
 
     def go(cp):
         cp.start()
@@ -123,14 +136,19 @@
             loaded(i)
         for cp in pending:
             cp.wait_send()
+        for cp in stores:
+            cp.wait()
 
     pl.semaphore_wait(bar, len(partners))
 
-    hop1 = [
-        go(send(states.at[:, rows(sections[m], RC)], b.layers.at[pl.ds(2 * s, 2)], b.h1_sem, m, sdev(m)))
-        for m in far_first
-    ]
-    loaded(0, 1, 2, 3)
+    hop1 = {}
+    for j in range(PIECES):
+        for m in far_first:
+            hop1[j, m] = go(send(
+                states.at[:, rows(sections[m], RC), piece(j)],
+                layers[j].at[pl.ds(2 * s, 2)], b.h1_sem, j * SEC + m, sdev(m),
+            ))
+    loaded(0, 1, 2, 3, 4)
     wanted = []
     for i in range(SEC):
         layer = jnp.int32(0)
@@ -150,15 +168,27 @@
         == lax.broadcasted_iota(jnp.int32, (HB, cfg.heads), 0) + d * HB
     )
     b.wstep[...] = dot(pick.astype(BF), b.wside[W:, :]).astype(BF)
-
-    for cp in hop1:
-        cp.wait_recv()
+    for j in range(F // 128):
+        b.win[128 * j: 128 * (j + 1), C:] = b.wside[:W, 128 * j: 128 * (j + 1)].T
+    loaded(9)
+    for i in range(C // 128):
+        for j in range(F // 128):
+            b.woutt[128 * j: 128 * (j + 1), 128 * i: 128 * (i + 1)] = (
+                b.wout[128 * i: 128 * (i + 1), 128 * j: 128 * (j + 1)].T
+            )
+
     mine = rows(core, RC)
-    b.src[zl, d, mine, :] = b.layers[layer_of[0]]
     hop2 = {}
-    for m in range(1, SEC):
-        b.stage[0, m] = b.layers[layer_of[m]]
-        hop2[m] = go(send(b.stage.at[0, m], b.src.at[zl, d, mine], b.h2_sem, m, sdev(m)))
+    for j in range(PIECES):
+        at = piece(j)
+        for m in far_first:
+            hop1[j, m].wait_recv()
+        b.src[zl, d, mine, at] = layers[j][layer_of[0]]
+        for m in range(1, SEC):
+            b.stage[0, m, :, at] = layers[j][layer_of[m]]
+            hop2[j, m] = go(send(
+                b.stage.at[0, m, :, at], b.src.at[zl, d, mine, at], b.h2_sem, j * SEC + m, sdev(m)
+            ))
 
     def g_copy(i, k):
         at = b.src.at[chips[i], d]
@@ -166,29 +196,22 @@
 
     for i in range(NC):
         for m in (2 * i, 2 * i + 1):
-            if m:
-                hop2[m].wait_recv()
+            for j in range(PIECES if m else 0):
+                hop2[j, m].wait_recv()
         for k in arrival(ND):
             go(g_copy(i, k))
     hop3 = []
     for m in range(1, SEC):
-        b.stage[1, m] = b.layers[jnp.minimum(layer_of[m] + 1, 2 * SEC - 1)]
+        for j in range(PIECES):
+            b.stage[1, m, :, piece(j)] = layers[j][jnp.minimum(layer_of[m] + 1, 2 * SEC - 1)]
         hop3.append(go(send(b.stage.at[1, m], b.tgt.at[rows(s, RC)], b.h3_sem, m, sdev(m))))
-    b.tgt[rows(s, RC), :] = b.layers[jnp.minimum(layer_of[0] + 1, 2 * SEC - 1)]
-    loaded(4)
-
-    NB = 256
-
-    def product(lhs, c, w, out, i, transposed=False):
-        def step(n, carry):
-            cols = pl.ds(pl.multiple_of(n * NB, NB), NB)
-            w_n = w[cols, :] if transposed else w[:, cols]
-            x = lhs[c].reshape(ND * CR, lhs.shape[3])
-            r = dot(x, w_n, 1, 1 if transposed else 0).astype(BF)
-            out[i, :, :, cols] = r.reshape(ND, CR, NB)
-            return carry
-
-        lax.fori_loop(0, (w.shape[0] if transposed else w.shape[1]) // NB, step, 0)
+    for j in range(PIECES):
+        b.tgt[rows(s, RC), piece(j)] = layers[j][jnp.minimum(layer_of[0] + 1, 2 * SEC - 1)]
+    loaded(5)
+
+    def product(lhs, c, w, out, i):
+        x = lhs[c].reshape(ND * CR, lhs.shape[3])
+        out[i] = dot(x, w[...]).astype(BF).reshape(ND, CR, w.shape[1])
 
     def c_copy(i, rel):
         q = (y + rel) % NY
@@ -202,8 +225,6 @@
             g_copy(i, k).wait_recv()
         c = chips[i]
         product(b.src, c, b.win, b.psend, i)
-        x = b.src[c].reshape(ND * CR, F)
-        b.psend[i, :, :, C:] = dot(x, b.wside[:W, :], 1, 1).astype(BF).reshape(ND, CR, W)
         for rel in arrival(NY):
             go(c_copy(i, rel))
 
@@ -230,8 +251,6 @@
 
     for i in range(NC):
         c_step(i)
-        if i:
-            c_sum(i - 1)
     for rel in arrival(NY) + [0]:
         x = b.src[:, (y + rel) % NY].reshape(T, F)
         b.stsend[rel] = dot(b.wstep[...], x, 1, 1).astype(BF)
@@ -242,14 +261,16 @@
             b.srct[128 * j: 128 * (j + 1), ND * CR * c: ND * CR * (c + 1)] = (
                 b.src[c, :, :, 128 * j: 128 * (j + 1)].reshape(ND * CR, 128).T
             )
-    c_sum(NC - 1)
+    write(b.srct, srct)
+    for i in range(NC):
+        c_sum(i)
     steps = b.stsend[0].astype(F32)
     for rel in range(1, NY):
         st_copy(rel).wait_recv()
         steps = steps + b.strec[rel].astype(F32)
     b.stz[0] = steps.astype(BF)
     stz = go(send(b.stz.at[0], b.stz.at[1], b.st_sem, NY, zdev))
-    loaded(5, 6, 7)
+    loaded(6, 7, 8)
     for i in range(NC):
         z_copy(i).wait_recv()
         here = rows(chips[i], CR)
@@ -325,7 +346,6 @@
                 spread_y(buf, sems, c, rel, which).wait_recv()
 
     spread(b.mix, b.e_sem)
-    loaded(8)
     spread_on(b.mix, b.e_sem)
 
     def f_copy(c, rel):
@@ -342,7 +362,7 @@
             b.mixt[128 * j: 128 * (j + 1), NY * CR * c: NY * CR * (c + 1)] = (
                 b.mix[c, :, :, 128 * j: 128 * (j + 1)].reshape(NY * CR, 128).T
             )
-    loaded(9)
+    loaded(10)
     for cp in hop3:
         cp.wait_recv()
     inner = layer_of[0] + 1 < 2 * SEC
@@ -391,7 +411,7 @@
     def i_step(c):
         for k in arrival(ND):
             h_copy(c, k).wait_recv()
-        product(b.og, c, b.wout, b.isend, c, transposed=True)
+        product(b.og, c, b.woutt, b.isend, c)
         for rel in arrival(NY):
             go(i_copy(c, rel))
 
@@ -411,8 +431,6 @@
 
     for c in range(NC):
         i_step(c)
-        if c:
-            i_sum(c - 1)
     total = b.lsum[0]
     for k in range(1, ND):
         loss_x(k).wait_recv()
@@ -420,14 +438,12 @@
     b.lsum[1] = total
     for k in range(1, NY):
         go(loss_y(k))
-    i_sum(NC - 1)
-
-    def store(n, carry):
-        at = pl.ds(pl.multiple_of(n * 256, 256), 256)
+    for c in range(NC):
+        i_sum(c)
+    for n in range(C // 256):
+        at = slice(256 * n, 256 * (n + 1))
         b.gout[at, :] = dot(b.mixt[at, :], b.og[...].reshape(ND * T, F)).astype(BF)
-        return carry
-
-    lax.fori_loop(0, C // 256, store, 0)
+    write(b.gout, g_out)
     total = b.lsum[1]
     for k in range(1, NY):
         loss_y(k).wait_recv()
@@ -438,6 +454,18 @@
         iz_copy(c).wait_recv()
         b.grad[CR * c: CR * (c + 1), :] += b.izrec[c].astype(F32)
 
+    def k_lanes(j, own):
+        return pl.ds(pl.multiple_of((zh if own else oz) * H + 128 * j, 128), 128)
+
+    def k_z(j):
+        at = b.vg.at[:, y, :, k_lanes(j, True)]
+        return send(at, at, b.k_sem, j, zdev)
+
+    def k_y(j, rel, which):
+        at = b.vg.at[:, y, :, k_lanes(j, not which)]
+        return send(at, at, b.k_sem, NJ + (2 * j + which) * NY + rel, ydev((y + rel) % NY))
+
+    NJ = H // 128
     dscore = jnp.zeros((T, T), F32)
     sums = []
     at_lane = lax.broadcasted_iota(jnp.int32, (T, 128), 1)
@@ -467,9 +495,9 @@
         b.vg[:, y, :, lanes(j)] = (
             (jnp.where(low, outs[0], outs[1]) + skips * g).astype(BF).reshape(NC, CR, 128)
         )
-    for c in range(NC):
+        go(k_z(j))
         for rel in arrival(NY):
-            go(spread_y(b.vg, b.k_sem, c, rel, 0))
+            go(k_y(j, rel, 0))
     dstep = jnp.concatenate(sums, axis=0)
     dcum = rowcols.T[:HH, :] - step * dstep
     ddecay = dot(dcum, causal.astype(F32), precision=HI)
@@ -481,8 +509,6 @@
     b.j1send[:W, :] = drw.astype(BF)
     b.j1send[W:, :] = dsteps.astype(BF)
     j1 = go(send(b.j1send, b.j1rec, b.iz_sem, NC, zdev))
-    for c in range(NC):
-        go(spread_z(b.vg, b.k_sem, c))
     j1.wait_recv()
     b.j2send[:W, :] = (drw + b.j1rec[:W, :].astype(F32)).astype(BF)
     b.j2send[W:, :] = (dsteps + b.j1rec[W:, :].astype(F32)).astype(BF)
@@ -493,7 +519,10 @@
 
     for k in arrival(ND):
         go(j2_copy(k))
-    spread_on(b.vg, b.k_sem)
+    for j in range(NJ):
+        k_z(j).wait_recv()
+        for rel in arrival(NY):
+            go(k_y(j, rel, 1))
     for k in arrival(ND):
         j2_copy(k).wait_recv()
     part = b.j2rec[0, :W, :].astype(F32)
@@ -512,33 +541,57 @@
     b.lout[...] = (
         jnp.zeros((8, 128), F32) + jnp.sum(b.lsum[2] + b.lrec[ND + NY]) / (T * ND * F * NY * NZ)
     )
-    stores = []
-
-    def write(src, dst):
-        cp = pltpu.make_async_copy(src, dst, b.store_sem.at[len(stores)])
-        cp.start()
-        stores.append(cp)
-
     write(b.lout, loss)
-    write(b.gout, g_out.at[0])
-    for c in range(NC):
-        spread_done(b.vg, b.k_sem, c)
-    w = min(256, F)
-    for n in range(F // w):
-        b.gin[w * n: w * (n + 1), :] = dot(
-            b.srct[w * n: w * (n + 1), :], b.vg[...].reshape(ND * T, C)
-        ).astype(BF)
-        write(b.gin.at[pl.ds(w * n, w)], g_in.at[0, pl.ds(w * n, w)])
+    for j in range(NJ):
+        for rel in arrival(NY):
+            for which in (0, 1):
+                k_y(j, rel, which).wait_recv()
+        for h in range(NZ):
+            at = pl.ds(h * H + 128 * j, 128)
+            write(b.vg.at[:, :, :, at], vg.at[:, :, :, at])
     for k in arrival(NY):
         j3_copy(k).wait_recv()
     out = jnp.zeros((W + cfg.heads, F), F32)
     for q in range(NY):
         out = out + dot(b.j3[q], b.src[:, q].reshape(T, F))
     b.gside[...] = out.astype(BF)
-    write(b.gside, g_side.at[0])
+    write(b.gside, g_side)
 
     finish()
-    for cp in stores:
+
+
+def last(srct, vg, side, out, loss, g_in, g_side, g_out, mean,
+         left, right, rows, means, sides, outs, sems):
+    n, block = rows.shape[0], rows.shape[1]
+    fetch = [
+        pltpu.make_async_copy(a, z, sems.at[i])
+        for i, (a, z) in enumerate((
+            (srct, left), (vg, right), (loss, means), (side, sides), (out, outs)
+        ))
+    ]
+    store = [
+        pltpu.make_async_copy(a, z.at[0], sems.at[len(fetch) + i])
+        for i, (a, z) in enumerate(((outs, g_out), (sides, g_side)))
+    ]
+    for cp in fetch:
+        cp.start()
+    for cp in fetch[:3]:
+        cp.wait()
+    mean[0] = jnp.max(means[...])
+    for i in range(n):
+        x = left[block * i: block * (i + 1), :]
+        rows[i] = dot(x, right[...].reshape(left.shape[1], right.shape[3])).astype(BF)
+        if i == 0:
+            fetch[4].wait()
+            store[0].start()
+            fetch[3].wait()
+            store[1].start()
+        cp = pltpu.make_async_copy(
+            rows.at[i], g_in.at[0, pl.ds(block * i, block)], sems.at[len(fetch) + 2 + i]
+        )
+        cp.start()
+        store.append(cp)
+    for cp in store:
         cp.wait()
 
 
@@ -555,7 +608,7 @@
     n = t * nd
     nc = sec // 2
     cr = t // nc
-    nstore = 3 + max(1, f // 256)
+    nstore = 4 + c // 128
     assert ny == nd and t == 128
     V, S = pltpu.VMEM, pltpu.SMEM
 
@@ -565,9 +618,9 @@
     scratch = dict(
         retained=S((sec,), jnp.int32), slot=S((sec,), jnp.int32),
         rate=S((1, heads), F32), bias=S((1, heads), F32), skip=S((1, heads), F32),
-        layers=V((2 * sec, t // sec, f), BF), stage=V((2, sec, t // sec, f), BF),
+        layers0=V((2 * sec, t // sec, f // 2), BF), layers1=V((2 * sec, t // sec, f // 2), BF), stage=V((2, sec, t // sec, f), BF),
         src=V((nc, nd, cr, f), BF), tgt=V((t, f), BF), final=V((t, f), BF), srct=V((f, n), BF),
-        win=V((f, c), BF), wside=V((sd, f), BF), wout=V((c, f), BF), wstep=V((hb, f), BF),
+        win=V((f, c + 2 * NS), BF), woutt=V((f, c), BF), wside=V((sd, f), BF), wout=V((c, f), BF), wstep=V((hb, f), BF),
         psend=V((nc, ny, cr, c + 2 * NS), BF), prec=V((nc, ny, cr, c + 2 * NS), BF),
         zsend=V((nc, cr, h + 2 * NS), BF), zrec=V((nc, cr, h + 2 * NS), BF),
         stsend=V((ny, hb, t), BF), strec=V((ny, hb, t), BF), stz=V((2, hb, t), BF),
@@ -580,36 +633,51 @@
         gout=V((c, f), BF), vg=V((nc, ny, cr, c), BF),
         j1send=V((side, t), BF), j1rec=V((side, t), BF),
         j2send=V((side, t), BF), j2rec=V((nd, side, t), BF), j3=V((ny, sd, t), BF),
-        gin=V((f, c), BF), gside=V((sd, f), BF),
-        load_sem=pltpu.SemaphoreType.DMA((10,)), store_sem=pltpu.SemaphoreType.DMA((nstore,)),
-        h1_sem=sems(sec), h2_sem=sems(sec), h3_sem=sems(sec), g_sem=sems(nc * nd),
+        gside=V((sd, f), BF),
+        load_sem=pltpu.SemaphoreType.DMA((11,)), store_sem=pltpu.SemaphoreType.DMA((nstore,)),
+        h1_sem=sems(2 * sec), h2_sem=sems(2 * sec), h3_sem=sems(sec), g_sem=sems(nc * nd),
         c_sem=sems(nc * ny), z_sem=sems(nc), st_sem=sems(ny + 1), e_sem=sems(nc + 2 * nc * ny),
         f_sem=sems(nc * nd), h_sem=sems(nc * nd), i_sem=sems(nc * ny), iz_sem=sems(nc + 1),
-        l_sem=sems(nd + ny + 1), k_sem=sems(nc + 2 * nc * ny), j2_sem=sems(nd), j3_sem=sems(ny),
+        l_sem=sems(nd + ny + 1), k_sem=sems(h // 128 * (1 + 2 * ny)), j2_sem=sems(nd), j3_sem=sems(ny),
     )
     cfg = SimpleNamespace(
         names=tuple(scratch), nd=nd, sec=sec, ny=ny, t=t, f=f, c=c, hb=hb, heads=heads
     )
-    hbm = pl.BlockSpec(memory_space=pltpu.HBM)
-    anywhere = pl.BlockSpec(memory_space=pl.ANY)
-    g_in, g_side, g_out, loss = pl.pallas_call(
+    hbm = pl.BlockSpec(memory_space=pl.ANY)
+    shape = jax.ShapeDtypeStruct
+    parts = pl.pallas_call(
         functools.partial(kernel, cfg, None),
         out_shape=(
-            jax.ShapeDtypeStruct(w_in.shape, BF), jax.ShapeDtypeStruct((1, sd, f), BF),
-            jax.ShapeDtypeStruct(w_out.shape, BF), jax.ShapeDtypeStruct((8, 128), F32),
+            shape((f, n), BF), shape((nc, ny, cr, c), BF), shape((sd, f), BF), shape((c, f), BF),
+            shape((8, 128), F32),
         ),
         in_specs=[hbm] * 10,
-        out_specs=(anywhere,) * 4,
+        out_specs=(hbm,) * 5,
         scratch_shapes=list(scratch.values()),
         compiler_params=pltpu.CompilerParams(
-            collective_id=0, has_side_effects=True, vmem_limit_bytes=36 << 20
+            collective_id=0, has_side_effects=True, vmem_limit_bytes=VMEM_BYTES
         ),
         name="distill",
     )(
         states, final_state, retained, block_slot, w_in, jnp.swapaxes(w_side, 1, 2), w_out,
         a_rate, dt_bias, skip,
     )
-    return g_in, jnp.swapaxes(g_side, 1, 2), g_out, loss[0, :1]
+    block = min(256, f)
+    g_in, g_side, g_out, mean = pl.pallas_call(
+        last,
+        out_shape=(
+            shape(w_in.shape, BF), shape((1, sd, f), BF), shape(w_out.shape, BF), shape((1,), F32)
+        ),
+        in_specs=[hbm] * 5,
+        out_specs=(hbm, hbm, hbm, pl.BlockSpec(memory_space=S)),
+        scratch_shapes=[
+            V((f, n), BF), V((nc, ny, cr, c), BF), V((f // block, block, c), BF), V((8, 128), F32),
+            V((sd, f), BF), V((c, f), BF), pltpu.SemaphoreType.DMA((7 + f // block,)),
+        ],
+        compiler_params=pltpu.CompilerParams(vmem_limit_bytes=VMEM_BYTES),
+        name="last",
+    )(*parts)
+    return g_in, jnp.swapaxes(g_side, 1, 2), g_out, mean
 
 
 def solution(mesh):

time: 137 us -> 124 us (0.905); the launches traced: 135 us -> 124 us
  local copies, waits for them, and re-layouts: 13.3 us -> 0 us
  Pallas kernels: 121 us -> 123 us
    unnamed x23 -> x0, local copies, waits for them, and re-layouts: 12.8 us -> none
    pallas_call x1 -> x2, Pallas kernels: 121 us -> 123 us  [the longest x1 118 us: local(): pl.pallas_call(functools.partial(kernel, cfg, None), out_shape=(shape((f,...]
where the time goes in v3:
time: 124 us
  Pallas kernels  123 us (99%)
    pallas_call x1, Pallas kernels, local(): pl.pallas_call(functools.partial(kernel, cfg, None), out_shape=(shape((f,...  118 us
    pallas_call x1, Pallas kernels, local(): pl.pallas_call(last, out_shape=(shape(w_in.shape, BF), shape((1, sd, f),...  5.1 us

profile of v3, /device:TPU:32, one launch (start us, length us, event | category | flops | bytes accessed | tf_op | source)
XLA Modules:
  0.0 123.8 jit_solution(16789654099358522077)
XLA Ops:
  0.6 118.0 %distill.1 = (bf16[1024,512]{1,0:T(8,128)(2,1)}, bf16[4,4,32,1024]{3,2,1,0:T(8,128)(2,1)}, bf16[192,1024]{1,0:T(8,128)(2,1)}, bf16[1024,1024]{1,0:T(8,128)(2,1)}, f32[8,128]{1,0:T(8,128)}) custom-call(bf16[2,128,1024]{2,1,0:T(8,128)(2,1)} %states.1, bf16[128,1024]{1,0:T(8,128)(2,1)} %final.1, s32[8]{0:T(128)} %retained.1, s32[8]{0:T(128)} %slot.1, ...), custom_call_target="tpu_custom_call" | custom-call | tf_op jit(solution)/shard_map/distill/pallas_call | solution.py:648
  118.7 5.1 %last.1 = (bf16[1,1024,1024]{2,1,0:T(8,128)(2,1)}, bf16[1,192,1024]{2,1,0:T(8,128)(2,1)}, bf16[1,1024,1024]{2,1,0:T(8,128)(2,1)}, f32[1]{0:T(128)}) custom-call(bf16[1024,512]{1,0:T(8,128)(2,1)} %get-tuple-element.13.srct, bf16[4,4,32,1024]{3,2,1,0:T(8,128)(2,1)} %get-tuple-element.14.vg, bf16[192,1024]{1,0:T(8,128)(2,1)} %get-tuple-element.15.side, ...), custom_call_target="tpu_custom_call" | custom-call | tf_op jit(solution)/shard_map/last/pallas_call | solution.py:666

commit v4 on v3

--- a/solution.py
+++ b/solution.py
@@ -11,6 +11,8 @@
 P_SIZE = 64
 NS = 64
 VMEM_BYTES = 60 << 20
+CHUNKS = (4, 8)
+LAGS = (4, 8, 8, 8)
 NZ = 2
 MESH = pl.DeviceIdType.MESH
 F32 = jnp.float32
@@ -39,13 +41,14 @@
 
 
 def kernel(cfg, stop, states, final, retained, slot, w_in, w_side, w_out, a_rate, dt_bias, skip,
-           srct, vg, g_side, g_out, loss, *scratch):
+           g_in, g_side, g_out, loss, *scratch):
     b = SimpleNamespace(**dict(zip(cfg.names, scratch)))
     ND, SEC, NY = cfg.nd, cfg.sec, cfg.ny
     T, F, C, H = cfg.t, cfg.f, cfg.c, cfg.c // NZ
     HB, HH = cfg.hb, cfg.hb // NZ
-    NC = SEC // 2
-    RC, CR = T // SEC, T // NC
+    NA, NB = cfg.na, cfg.nb
+    RC, CA, CB = T // SEC, T // NA, T // NB
+    PC = SEC // NA
     W = 2 * NS
     d, s, t = lax.axis_index("dp"), lax.axis_index("section"), lax.axis_index("tensor")
     zh, y = t // NY, t % NY
@@ -60,11 +63,12 @@
 
     zdev = (d, s, oz * NY + y)
 
-    if NC == 4:
+    if SEC == 8:
         chips = [zl, zl + 1 - 2 * (zl % 2), (zl + 2) % 4, 3 - zl]
     else:
         chips = [zl, 1 - zl]
     sections = [2 * c + k for c in chips for k in (core, 1 - core)]
+    chunks = [i // PC for i in sections[::PC]]
     far_first = [m for i in (2, 3, 1, 0) for m in (2 * i, 2 * i + 1) if 0 < m < SEC]
 
     def sdev(m):
@@ -177,25 +181,25 @@
                 b.wout[128 * i: 128 * (i + 1), 128 * j: 128 * (j + 1)].T
             )
 
-    mine = rows(core, RC)
+    mine = rows(s % PC, RC)
     hop2 = {}
     for j in range(PIECES):
         at = piece(j)
         for m in far_first:
             hop1[j, m].wait_recv()
-        b.src[zl, d, mine, at] = layers[j][layer_of[0]]
+        b.src[s // PC, d, mine, at] = layers[j][layer_of[0]]
         for m in range(1, SEC):
             b.stage[0, m, :, at] = layers[j][layer_of[m]]
             hop2[j, m] = go(send(
-                b.stage.at[0, m, :, at], b.src.at[zl, d, mine, at], b.h2_sem, j * SEC + m, sdev(m)
+                b.stage.at[0, m, :, at], b.src.at[s // PC, d, mine, at], b.h2_sem, j * SEC + m, sdev(m)
             ))
 
     def g_copy(i, k):
-        at = b.src.at[chips[i], d]
+        at = b.src.at[chunks[i], d]
         return send(at, at, b.g_sem, i * ND + k, xdev((d + k) % ND))
 
-    for i in range(NC):
-        for m in (2 * i, 2 * i + 1):
+    for i in range(NA):
+        for m in range(PC * i, PC * (i + 1)):
             for j in range(PIECES if m else 0):
                 hop2[j, m].wait_recv()
         for k in arrival(ND):
@@ -210,8 +214,8 @@
     loaded(5)
 
     def product(lhs, c, w, out, i):
-        x = lhs[c].reshape(ND * CR, lhs.shape[3])
-        out[i] = dot(x, w[...]).astype(BF).reshape(ND, CR, w.shape[1])
+        x = lhs[c].reshape(ND * lhs.shape[2], lhs.shape[3])
+        out[i] = dot(x, w[...]).astype(BF).reshape(ND, lhs.shape[2], w.shape[1])
 
     def c_copy(i, rel):
         q = (y + rel) % NY
@@ -223,7 +227,7 @@
     def c_step(i):
         for k in arrival(ND):
             g_copy(i, k).wait_recv()
-        c = chips[i]
+        c = chunks[i]
         product(b.src, c, b.win, b.psend, i)
         for rel in arrival(NY):
             go(c_copy(i, rel))
@@ -242,28 +246,24 @@
         side = total(slice(C, C + W))
         b.zsend[i, :, H:] = side.astype(BF)
         go(z_copy(i))
-        here = rows(chips[i], CR)
+        here = rows(chunks[i], CA)
         b.vals[here, :] = total(half(zh))
         b.rw[here, :] = side
 
     def st_copy(rel):
         return send(b.stsend.at[rel], b.strec.at[rel], b.st_sem, rel, ydev((y + rel) % NY))
 
-    for i in range(NC):
-        c_step(i)
+    for i in range(NA - 1 + LAGS[0]):
+        if i < NA:
+            c_step(i)
+        if 0 <= i - LAGS[0] < NA - 1:
+            c_sum(i - LAGS[0])
     for rel in arrival(NY) + [0]:
         x = b.src[:, (y + rel) % NY].reshape(T, F)
         b.stsend[rel] = dot(b.wstep[...], x, 1, 1).astype(BF)
         if rel:
             go(st_copy(rel))
-    for c in range(NC):
-        for j in range(F // 128):
-            b.srct[128 * j: 128 * (j + 1), ND * CR * c: ND * CR * (c + 1)] = (
-                b.src[c, :, :, 128 * j: 128 * (j + 1)].reshape(ND * CR, 128).T
-            )
-    write(b.srct, srct)
-    for i in range(NC):
-        c_sum(i)
+    c_sum(NA - 1)
     steps = b.stsend[0].astype(F32)
     for rel in range(1, NY):
         st_copy(rel).wait_recv()
@@ -271,9 +271,9 @@
     b.stz[0] = steps.astype(BF)
     stz = go(send(b.stz.at[0], b.stz.at[1], b.st_sem, NY, zdev))
     loaded(6, 7, 8)
-    for i in range(NC):
+    for i in range(NA):
         z_copy(i).wait_recv()
-        here = rows(chips[i], CR)
+        here = rows(chunks[i], CA)
         b.vals[here, :] += b.zrec[i, :, :H].astype(F32)
         b.rw[here, :] += b.zrec[i, :, H:].astype(F32)
     stz.wait_recv()
@@ -318,7 +318,7 @@
         y2 = jnp.where(low, outs[0], outs[1])
         b.pure[:, cols] = y2
         skips = jnp.where(low, b.skip[0, head0 + 2 * j], b.skip[0, head0 + 2 * j + 1])
-        b.mix[:, y, :, lanes(j)] = (y2 + skips * v).astype(BF).reshape(NC, CR, 128)
+        b.mix[:, y, :, lanes(j)] = (y2 + skips * v).astype(BF).reshape(NB, CB, 128)
 
     def spread_z(buf, sems, c):
         at = buf.at[c, y, :, half(zh)]
@@ -326,16 +326,16 @@
 
     def spread_y(buf, sems, c, rel, which):
         at = buf.at[c, y, :, half(oz if which else zh)]
-        return send(at, at, sems, NC + (2 * c + which) * NY + rel, ydev((y + rel) % NY))
+        return send(at, at, sems, NB + (2 * c + which) * NY + rel, ydev((y + rel) % NY))
 
     def spread(buf, sems):
-        for c in range(NC):
+        for c in range(NB):
             go(spread_z(buf, sems, c))
             for rel in arrival(NY):
                 go(spread_y(buf, sems, c, rel, 0))
 
     def spread_on(buf, sems):
-        for c in range(NC):
+        for c in range(NB):
             spread_z(buf, sems, c).wait_recv()
             for rel in arrival(NY):
                 go(spread_y(buf, sems, c, rel, 1))
@@ -352,85 +352,114 @@
         q = (d + rel) % ND
         return send(b.osend.at[c, q], b.orec.at[c, rel], b.f_sem, c * ND + rel, xdev(q))
 
-    for c in range(NC):
+    inner = layer_of[0] + 1 < 2 * SEC
+
+    def h_copy(c, k):
+        at = b.og.at[c, d]
+        return send(at, at, b.h_sem, c * ND + k, xdev((d + k) % ND))
+
+
+    def loss_x(k):
+        return send(b.lsum.at[0], b.lrec.at[k], b.l_sem, k, xdev((d + k) % ND))
+
+    def loss_y(k):
+        return send(b.lsum.at[1], b.lrec.at[ND + k], b.l_sem, ND + k, ydev((y + k) % NY))
+
+    def loss_z():
+        return send(b.lsum.at[2], b.lrec.at[ND + NY], b.l_sem, ND + NY, zdev)
+
+    def i_copy(c, rel):
+        q = (y + rel) % NY
+        return send(b.isend.at[c, q], b.irec.at[c, rel], b.i_sem, c * NY + rel, ydev(q))
+
+    def iz_copy(c):
+        return send(b.izsend.at[c], b.izrec.at[c], b.iz_sem, c, zdev)
+
+    def i_step(c):
+        for k in arrival(ND):
+            h_copy(c, k).wait_recv()
+        product(b.og, c, b.woutt, b.isend, c)
+        for rel in arrival(NY):
+            go(i_copy(c, rel))
+
+    def i_sum(c):
+        for rel in range(1, NY):
+            i_copy(c, rel).wait_recv()
+
+        def total(cols):
+            out = b.isend[c, y, :, cols].astype(F32)
+            for rel in range(1, NY):
+                out = out + b.irec[c, rel, :, cols].astype(F32)
+            return out
+
+        b.izsend[c] = total(half(oz)).astype(BF)
+        go(iz_copy(c))
+        b.grad[CB * c: CB * (c + 1), :] = total(half(zh))
+
+    def f_step(c):
         spread_done(b.mix, b.e_sem, c)
         product(b.mix, c, b.wout, b.osend, c)
         for rel in arrival(ND):
             go(f_copy(c, rel))
-    for c in range(NC):
-        for j in range(C // 128):
-            b.mixt[128 * j: 128 * (j + 1), NY * CR * c: NY * CR * (c + 1)] = (
-                b.mix[c, :, :, 128 * j: 128 * (j + 1)].reshape(NY * CR, 128).T
-            )
-    loaded(10)
-    for cp in hop3:
-        cp.wait_recv()
-    inner = layer_of[0] + 1 < 2 * SEC
-
-    def h_copy(c, k):
-        at = b.og.at[c, d]
-        return send(at, at, b.h_sem, c * ND + k, xdev((d + k) % ND))
-
-    total = jnp.zeros((8, 128), F32)
-    for c in range(NC):
+
+    def err_step(c):
+        total = jnp.zeros((8, 128), F32)
         for rel in range(1, ND):
             f_copy(c, rel).wait_recv()
         for j in range(F // 128):
             cols = slice(128 * j, 128 * (j + 1))
-            here = slice(CR * c, CR * (c + 1))
+            here = slice(CB * c, CB * (c + 1))
             out = b.osend[c, d, :, cols].astype(F32)
             for rel in range(1, ND):
                 out = out + b.orec[c, rel, :, cols].astype(F32)
             goal = jnp.where(inner, b.tgt[here, cols].astype(F32), b.final[here, cols].astype(F32))
             err = out - goal
             b.og[c, d, :, cols] = (2.0 * err / (T * ND)).astype(BF)
-            total = total + jnp.sum((err * err).reshape(CR // 8, 8, 128), axis=0)
+            total = total + jnp.sum((err * err).reshape(CB // 8, 8, 128), axis=0)
         for k in arrival(ND):
             go(h_copy(c, k))
-    b.lsum[0] = total
-
-    def loss_x(k):
-        return send(b.lsum.at[0], b.lrec.at[k], b.l_sem, k, xdev((d + k) % ND))
-
-    def loss_y(k):
-        return send(b.lsum.at[1], b.lrec.at[ND + k], b.l_sem, ND + k, ydev((y + k) % NY))
-
-    def loss_z():
-        return send(b.lsum.at[2], b.lrec.at[ND + NY], b.l_sem, ND + NY, zdev)
-
-    for k in range(1, ND):
-        go(loss_x(k))
-
-    def i_copy(c, rel):
-        q = (y + rel) % NY
-        return send(b.isend.at[c, q], b.irec.at[c, rel], b.i_sem, c * NY + rel, ydev(q))
-
-    def iz_copy(c):
-        return send(b.izsend.at[c], b.izrec.at[c], b.iz_sem, c, zdev)
-
-    def i_step(c):
-        for k in arrival(ND):
-            h_copy(c, k).wait_recv()
-        product(b.og, c, b.woutt, b.isend, c)
-        for rel in arrival(NY):
-            go(i_copy(c, rel))
-
-    def i_sum(c):
-        for rel in range(1, NY):
-            i_copy(c, rel).wait_recv()
-
-        def total(cols):
-            out = b.isend[c, y, :, cols].astype(F32)
-            for rel in range(1, NY):
-                out = out + b.irec[c, rel, :, cols].astype(F32)
-            return out
-
-        b.izsend[c] = total(half(oz)).astype(BF)
-        go(iz_copy(c))
-        b.grad[CR * c: CR * (c + 1), :] = total(half(zh))
-
-    for c in range(NC):
-        i_step(c)
+        return total
+
+    def prepare():
+        for c in range(NB):
+            for j in range(C // 128):
+                b.mixt[128 * j: 128 * (j + 1), NY * CB * c: NY * CB * (c + 1)] = (
+                    b.mix[c, :, :, 128 * j: 128 * (j + 1)].reshape(NY * CB, 128).T
+                )
+        for c in range(NA):
+            for j in range(F // 128):
+                b.srct[128 * j: 128 * (j + 1), ND * CA * c: ND * CA * (c + 1)] = (
+                    b.src[c, :, :, 128 * j: 128 * (j + 1)].reshape(ND * CA, 128).T
+                )
+        for k in range(HH):
+            decay, st = b.decay[k], step[k: k + 1, :]
+            both = decay * scores
+            b.both[k] = both
+            b.wt[k] = (both * st).T.astype(BF)
+            b.decay[k] = decay * st
+            cols = slice(128 * (k // 2), 128 * (k // 2 + 1))
+            b.vmask[k] = jnp.where(low if k % 2 == 0 else jnp.logical_not(low), b.vals[:, cols], 0.0).astype(BF)
+
+    loaded(10)
+    for cp in hop3:
+        cp.wait_recv()
+    total = jnp.zeros((8, 128), F32)
+    order = tuple(min(k, NB) for k in LAGS[1:])
+    for i in range(NB + sum(order)):
+        if i < NB:
+            f_step(i)
+        if i == NB - 1:
+            prepare()
+        if 0 <= i - order[0] < NB:
+            total = total + err_step(i - order[0])
+        if i - order[0] == NB - 1:
+            b.lsum[0] = total
+            for k in range(1, ND):
+                go(loss_x(k))
+        if 0 <= i - sum(order[:2]) < NB:
+            i_step(i - sum(order[:2]))
+        if 0 <= i - sum(order) < NB:
+            i_sum(i - sum(order))
     total = b.lsum[0]
     for k in range(1, ND):
         loss_x(k).wait_recv()
@@ -438,8 +467,6 @@
     b.lsum[1] = total
     for k in range(1, NY):
         go(loss_y(k))
-    for c in range(NC):
-        i_sum(c)
     for n in range(C // 256):
         at = slice(256 * n, 256 * (n + 1))
         b.gout[at, :] = dot(b.mixt[at, :], b.og[...].reshape(ND * T, F)).astype(BF)
@@ -450,9 +477,9 @@
         total = total + b.lrec[ND + k]
     b.lsum[2] = total
     go(loss_z())
-    for c in range(NC):
+    for c in range(NB):
         iz_copy(c).wait_recv()
-        b.grad[CR * c: CR * (c + 1), :] += b.izrec[c].astype(F32)
+        b.grad[CB * c: CB * (c + 1), :] += b.izrec[c].astype(F32)
 
     def k_lanes(j, own):
         return pl.ds(pl.multiple_of((zh if own else oz) * H + 128 * j, 128), 128)
@@ -466,6 +493,18 @@
         return send(at, at, b.k_sem, NJ + (2 * j + which) * NY + rel, ydev((y + rel) % NY))
 
     NJ = H // 128
+    for j in range(H // 128):
+        cols = slice(128 * j, 128 * (j + 1))
+        g = b.grad[:, cols]
+        gb = g.astype(BF)
+        outs = [dot(b.wt[2 * j + e], gb) for e in (0, 1)]
+        skips = jnp.where(low, b.skip[0, head0 + 2 * j], b.skip[0, head0 + 2 * j + 1])
+        b.vg[:, y, :, lanes(j)] = (
+            (jnp.where(low, outs[0], outs[1]) + skips * g).astype(BF).reshape(NA, CA, 128)
+        )
+        go(k_z(j))
+        for rel in arrival(NY):
+            go(k_y(j, rel, 0))
     dscore = jnp.zeros((T, T), F32)
     sums = []
     at_lane = lax.broadcasted_iota(jnp.int32, (T, 128), 1)
@@ -474,41 +513,32 @@
         cols = slice(128 * j, 128 * (j + 1))
         g = b.grad[:, cols]
         gb = g.astype(BF)
-        v = b.vals[:, cols]
         prod = g * b.pure[:, cols]
-        outs = []
         for e in (0, 1):
             k = 2 * j + e
             here = low if e == 0 else jnp.logical_not(low)
-            x = dot(gb, jnp.where(here, v, 0.0).astype(BF), 1, 1)
-            decay = b.decay[k]
-            st = step[k: k + 1, :]
-            xd = x * decay
-            dscore = dscore + xd * st
-            sums.append(jnp.sum(xd * scores, axis=0, keepdims=True))
+            x = dot(gb, b.vmask[k], 1, 1)
+            dscore = dscore + x * b.decay[k]
+            sums.append(jnp.sum(x * b.both[k], axis=0, keepdims=True))
             rowcols = jnp.where(
                 at_lane == k, jnp.sum(jnp.where(here, prod, 0.0), axis=1, keepdims=True), rowcols
             )
-            wt = (decay * scores * st).T.astype(BF)
-            outs.append(dot(wt, gb))
-        skips = jnp.where(low, b.skip[0, head0 + 2 * j], b.skip[0, head0 + 2 * j + 1])
-        b.vg[:, y, :, lanes(j)] = (
-            (jnp.where(low, outs[0], outs[1]) + skips * g).astype(BF).reshape(NC, CR, 128)
-        )
-        go(k_z(j))
-        for rel in arrival(NY):
-            go(k_y(j, rel, 0))
     dstep = jnp.concatenate(sums, axis=0)
     dcum = rowcols.T[:HH, :] - step * dstep
     ddecay = dot(dcum, causal.astype(F32), precision=HI)
+    wrb = wr.astype(BF)
     draw = (dstep - rate * ddecay) * jax.nn.sigmoid(raw)
-    drw = jnp.where(low, dot(dscore.T, wr, precision=HI), dot(dscore, wr, precision=HI)).T
+    drw = jnp.where(low, dot(dscore.T.astype(BF), wrb), dot(dscore.astype(BF), wrb)).T
     in_half = lax.broadcasted_iota(jnp.int32, (HB, T), 0) // HH == zh
     dsteps = jnp.where(in_half, jnp.concatenate([draw] * NZ, axis=0), 0.0)
 
     b.j1send[:W, :] = drw.astype(BF)
     b.j1send[W:, :] = dsteps.astype(BF)
-    j1 = go(send(b.j1send, b.j1rec, b.iz_sem, NC, zdev))
+    j1 = go(send(b.j1send, b.j1rec, b.iz_sem, NB, zdev))
+    for j in range(NJ):
+        k_z(j).wait_recv()
+        for rel in arrival(NY):
+            go(k_y(j, rel, 1))
     j1.wait_recv()
     b.j2send[:W, :] = (drw + b.j1rec[:W, :].astype(F32)).astype(BF)
     b.j2send[W:, :] = (dsteps + b.j1rec[W:, :].astype(F32)).astype(BF)
@@ -519,10 +549,6 @@
 
     for k in arrival(ND):
         go(j2_copy(k))
-    for j in range(NJ):
-        k_z(j).wait_recv()
-        for rel in arrival(NY):
-            go(k_y(j, rel, 1))
     for k in arrival(ND):
         j2_copy(k).wait_recv()
     part = b.j2rec[0, :W, :].astype(F32)
@@ -546,9 +572,12 @@
         for rel in arrival(NY):
             for which in (0, 1):
                 k_y(j, rel, which).wait_recv()
-        for h in range(NZ):
-            at = pl.ds(h * H + 128 * j, 128)
-            write(b.vg.at[:, :, :, at], vg.at[:, :, :, at])
+        halves = [slice(h * H + 128 * j, h * H + 128 * (j + 1)) for h in range(NZ)]
+        vg = jnp.concatenate([b.vg[:, :, :, at].reshape(ND * T, 128) for at in halves], axis=1)
+        part = dot(b.srct[...], vg).astype(BF)
+        for h, at in enumerate(halves):
+            b.gin[:, at] = part[:, 128 * h: 128 * (h + 1)]
+            write(b.gin.at[:, at], g_in.at[:, at])
     for k in arrival(NY):
         j3_copy(k).wait_recv()
     out = jnp.zeros((W + cfg.heads, F), F32)
@@ -560,37 +589,29 @@
     finish()
 
 
-def last(srct, vg, side, out, loss, g_in, g_side, g_out, mean,
-         left, right, rows, means, sides, outs, sems):
-    n, block = rows.shape[0], rows.shape[1]
+def last(side, out, inn, loss, g_side, g_out, g_in, mean, sides, outs, inns, means, sems):
+    moves = []
+    for a, v, z in ((out, outs, g_out), (inn, inns, g_in), (side, sides, g_side)):
+        n = a.shape[0]
+        size = max(n // 4, 64)
+        for i in range(n // size):
+            moves.append((a, v, z, pl.ds(size * i, size)))
     fetch = [
-        pltpu.make_async_copy(a, z, sems.at[i])
-        for i, (a, z) in enumerate((
-            (srct, left), (vg, right), (loss, means), (side, sides), (out, outs)
-        ))
+        pltpu.make_async_copy(a.at[at], v.at[at], sems.at[0, i])
+        for i, (a, v, z, at) in enumerate(moves)
     ]
     store = [
-        pltpu.make_async_copy(a, z.at[0], sems.at[len(fetch) + i])
-        for i, (a, z) in enumerate(((outs, g_out), (sides, g_side)))
+        pltpu.make_async_copy(v.at[at], z.at[0, at], sems.at[1, i])
+        for i, (a, v, z, at) in enumerate(moves)
     ]
-    for cp in fetch:
+    whole = pltpu.make_async_copy(loss, means, sems.at[0, len(moves)])
+    for cp in fetch + [whole]:
         cp.start()
-    for cp in fetch[:3]:
-        cp.wait()
+    for f, z in zip(fetch, store):
+        f.wait()
+        z.start()
+    whole.wait()
     mean[0] = jnp.max(means[...])
-    for i in range(n):
-        x = left[block * i: block * (i + 1), :]
-        rows[i] = dot(x, right[...].reshape(left.shape[1], right.shape[3])).astype(BF)
-        if i == 0:
-            fetch[4].wait()
-            store[0].start()
-            fetch[3].wait()
-            store[1].start()
-        cp = pltpu.make_async_copy(
-            rows.at[i], g_in.at[0, pl.ds(block * i, block)], sems.at[len(fetch) + 2 + i]
-        )
-        cp.start()
-        store.append(cp)
     for cp in store:
         cp.wait()
 
@@ -603,12 +624,12 @@
     heads = a_rate.shape[1]
     hb = c // P_SIZE
     sd = 2 * NS + heads
-    side = 2 * NS + hb
+    sr = 2 * NS + hb
     h = c // NZ
     n = t * nd
-    nc = sec // 2
-    cr = t // nc
-    nstore = 4 + c // 128
+    na, nb = min(CHUNKS[0], sec), CHUNKS[1]
+    ca, cb = t // na, t // nb
+    nstore = 3 + c // 128
     assert ny == nd and t == 128
     V, S = pltpu.VMEM, pltpu.SMEM
 
@@ -619,40 +640,40 @@
         retained=S((sec,), jnp.int32), slot=S((sec,), jnp.int32),
         rate=S((1, heads), F32), bias=S((1, heads), F32), skip=S((1, heads), F32),
         layers0=V((2 * sec, t // sec, f // 2), BF), layers1=V((2 * sec, t // sec, f // 2), BF), stage=V((2, sec, t // sec, f), BF),
-        src=V((nc, nd, cr, f), BF), tgt=V((t, f), BF), final=V((t, f), BF), srct=V((f, n), BF),
+        src=V((na, nd, ca, f), BF), tgt=V((t, f), BF), final=V((t, f), BF), srct=V((f, n), BF),
         win=V((f, c + 2 * NS), BF), woutt=V((f, c), BF), wside=V((sd, f), BF), wout=V((c, f), BF), wstep=V((hb, f), BF),
-        psend=V((nc, ny, cr, c + 2 * NS), BF), prec=V((nc, ny, cr, c + 2 * NS), BF),
-        zsend=V((nc, cr, h + 2 * NS), BF), zrec=V((nc, cr, h + 2 * NS), BF),
+        psend=V((na, ny, ca, c + 2 * NS), BF), prec=V((na, ny, ca, c + 2 * NS), BF),
+        zsend=V((na, ca, h + 2 * NS), BF), zrec=V((na, ca, h + 2 * NS), BF),
         stsend=V((ny, hb, t), BF), strec=V((ny, hb, t), BF), stz=V((2, hb, t), BF),
         steps=V((hb, t), F32), rw=V((t, 2 * NS), F32), vals=V((t, h), F32), pure=V((t, h), F32),
-        decay=V((hb // NZ, t, t), F32), mix=V((nc, ny, cr, c), BF), mixt=V((c, n), BF),
-        osend=V((nc, nd, cr, f), BF), orec=V((nc, nd, cr, f), BF), og=V((nc, nd, cr, f), BF),
+        decay=V((hb // NZ, t, t), F32), both=V((hb // NZ, t, t), F32),
+        wt=V((hb // NZ, t, t), BF), vmask=V((hb // NZ, t, t), BF), mix=V((nb, ny, cb, c), BF), mixt=V((c, n), BF),
+        osend=V((nb, nd, cb, f), BF), orec=V((nb, nd, cb, f), BF), og=V((nb, nd, cb, f), BF),
         lsum=V((3, 8, 128), F32), lrec=V((nd + ny + 1, 8, 128), F32), lout=V((8, 128), F32),
-        isend=V((nc, ny, cr, c), BF), irec=V((nc, ny, cr, c), BF),
-        izsend=V((nc, cr, h), BF), izrec=V((nc, cr, h), BF), grad=V((t, h), F32),
-        gout=V((c, f), BF), vg=V((nc, ny, cr, c), BF),
-        j1send=V((side, t), BF), j1rec=V((side, t), BF),
-        j2send=V((side, t), BF), j2rec=V((nd, side, t), BF), j3=V((ny, sd, t), BF),
+        isend=V((nb, ny, cb, c), BF), irec=V((nb, ny, cb, c), BF),
+        izsend=V((nb, cb, h), BF), izrec=V((nb, cb, h), BF), grad=V((t, h), F32),
+        gout=V((c, f), BF), gin=V((f, c), BF), vg=V((na, ny, ca, c), BF),
+        j1send=V((sr, t), BF), j1rec=V((sr, t), BF),
+        j2send=V((sr, t), BF), j2rec=V((nd, sr, t), BF), j3=V((ny, sd, t), BF),
         gside=V((sd, f), BF),
         load_sem=pltpu.SemaphoreType.DMA((11,)), store_sem=pltpu.SemaphoreType.DMA((nstore,)),
-        h1_sem=sems(2 * sec), h2_sem=sems(2 * sec), h3_sem=sems(sec), g_sem=sems(nc * nd),
-        c_sem=sems(nc * ny), z_sem=sems(nc), st_sem=sems(ny + 1), e_sem=sems(nc + 2 * nc * ny),
-        f_sem=sems(nc * nd), h_sem=sems(nc * nd), i_sem=sems(nc * ny), iz_sem=sems(nc + 1),
+        h1_sem=sems(2 * sec), h2_sem=sems(2 * sec), h3_sem=sems(sec), g_sem=sems(na * nd),
+        c_sem=sems(na * ny), z_sem=sems(na), st_sem=sems(ny + 1), e_sem=sems(nb + 2 * nb * ny),
+        f_sem=sems(nb * nd), h_sem=sems(nb * nd), i_sem=sems(nb * ny), iz_sem=sems(nb + 1),
         l_sem=sems(nd + ny + 1), k_sem=sems(h // 128 * (1 + 2 * ny)), j2_sem=sems(nd), j3_sem=sems(ny),
     )
     cfg = SimpleNamespace(
-        names=tuple(scratch), nd=nd, sec=sec, ny=ny, t=t, f=f, c=c, hb=hb, heads=heads
+        names=tuple(scratch), nd=nd, sec=sec, ny=ny, t=t, f=f, c=c, hb=hb, heads=heads, na=na, nb=nb
     )
     hbm = pl.BlockSpec(memory_space=pl.ANY)
     shape = jax.ShapeDtypeStruct
-    parts = pl.pallas_call(
+    inn, side, out, loss = pl.pallas_call(
         functools.partial(kernel, cfg, None),
         out_shape=(
-            shape((f, n), BF), shape((nc, ny, cr, c), BF), shape((sd, f), BF), shape((c, f), BF),
-            shape((8, 128), F32),
+            shape((f, c), BF), shape((sd, f), BF), shape((c, f), BF), shape((8, 128), F32),
         ),
         in_specs=[hbm] * 10,
-        out_specs=(hbm,) * 5,
+        out_specs=(hbm,) * 4,
         scratch_shapes=list(scratch.values()),
         compiler_params=pltpu.CompilerParams(
             collective_id=0, has_side_effects=True, vmem_limit_bytes=VMEM_BYTES
@@ -662,21 +683,20 @@
         states, final_state, retained, block_slot, w_in, jnp.swapaxes(w_side, 1, 2), w_out,
         a_rate, dt_bias, skip,
     )
-    block = min(256, f)
-    g_in, g_side, g_out, mean = pl.pallas_call(
+    g_side, g_out, g_in, mean = pl.pallas_call(
         last,
         out_shape=(
-            shape(w_in.shape, BF), shape((1, sd, f), BF), shape(w_out.shape, BF), shape((1,), F32)
+            shape((1, sd, f), BF), shape(w_out.shape, BF), shape(w_in.shape, BF), shape((1,), F32)
         ),
-        in_specs=[hbm] * 5,
+        in_specs=[hbm] * 4,
         out_specs=(hbm, hbm, hbm, pl.BlockSpec(memory_space=S)),
         scratch_shapes=[
-            V((f, n), BF), V((nc, ny, cr, c), BF), V((f // block, block, c), BF), V((8, 128), F32),
-            V((sd, f), BF), V((c, f), BF), pltpu.SemaphoreType.DMA((7 + f // block,)),
+            V((sd, f), BF), V((c, f), BF), V((f, c), BF), V((8, 128), F32),
+            pltpu.SemaphoreType.DMA((2, 16)),
         ],
         compiler_params=pltpu.CompilerParams(vmem_limit_bytes=VMEM_BYTES),
         name="last",
-    )(*parts)
+    )(side, out, inn, loss)
     return g_in, jnp.swapaxes(g_side, 1, 2), g_out, mean
 
 

time: 124 us -> 122 us (0.984)
  Pallas kernels: 123 us -> 121 us
where the time goes in v4:
time: 122 us
  Pallas kernels  121 us (99%)
    pallas_call x1, Pallas kernels, local(): pl.pallas_call(functools.partial(kernel, cfg, None), out_shape=(shape((f,...  117 us
    pallas_call x1, Pallas kernels, local(): pl.pallas_call(last, out_shape=(shape((1, sd, f), BF), shape(w_out.shape,...  4.5 us

profile of v4, /device:TPU:32, one launch (start us, length us, event | category | flops | bytes accessed | tf_op | source)
XLA Modules:
  0.0 122.3 jit_solution(385607214813692589)
XLA Ops:
  0.6 117.0 %distill.1 = (bf16[1024,1024]{1,0:T(8,128)(2,1)}, bf16[192,1024]{1,0:T(8,128)(2,1)}, bf16[1024,1024]{1,0:T(8,128)(2,1)}, f32[8,128]{1,0:T(8,128)}) custom-call(bf16[2,128,1024]{2,1,0:T(8,128)(2,1)} %states.1, bf16[128,1024]{1,0:T(8,128)(2,1)} %final.1, s32[8]{0:T(128)} %retained.1, s32[8]{0:T(128)} %slot.1, bf16[1,1024,1024]{2,1,0:T(8,128)(2,1)} %w_in.1, ...), custom_call_target="tpu_custom_call" | custom-call | tf_op jit(solution)/shard_map/distill/pallas_call | solution.py:670
  117.6 4.5 %last.1 = (bf16[1,192,1024]{2,1,0:T(8,128)(2,1)}, bf16[1,1024,1024]{2,1,0:T(8,128)(2,1)}, bf16[1,1024,1024]{2,1,0:T(8,128)(2,1)}, f32[1]{0:T(128)}) custom-call(bf16[192,1024]{1,0:T(8,128)(2,1)} %get-tuple-element.12.side, bf16[1024,1024]{1,0:T(8,128)(2,1)} %get-tuple-element.13.out, bf16[1024,1024]{1,0:T(8,128)(2,1)} %get-tuple-element.14.inn, ...), custom_call_target="tpu_custom_call" | custom-call | tf_op jit(solution)/shard_map/last/pallas_call | solution.py:686

commit v5 on v4

--- a/solution.py
+++ b/solution.py
@@ -331,6 +331,7 @@
     def spread(buf, sems):
         for c in range(NB):
             go(spread_z(buf, sems, c))
+        for c in range(NB):
             for rel in arrival(NY):
                 go(spread_y(buf, sems, c, rel, 0))
 

time: 122 us -> 122 us (level)
  no operation moved by 1% of the time
where the time goes in v5:
time: 122 us
  Pallas kernels  122 us (100%)
    pallas_call x1, Pallas kernels, local(): pl.pallas_call(functools.partial(kernel, cfg, None), out_shape=(shape((f,...  117 us
    pallas_call x1, Pallas kernels, local(): pl.pallas_call(last, out_shape=(shape((1, sd, f), BF), shape(w_out.shape,...  4.5 us

profile of v5, /device:TPU:32, one launch (start us, length us, event | category | flops | bytes accessed | tf_op | source)
XLA Modules:
  0.0 122.3 jit_solution(9179550503755501309)
XLA Ops:
  0.6 117.0 %distill.1 = (bf16[1024,1024]{1,0:T(8,128)(2,1)}, bf16[192,1024]{1,0:T(8,128)(2,1)}, bf16[1024,1024]{1,0:T(8,128)(2,1)}, f32[8,128]{1,0:T(8,128)}) custom-call(bf16[2,128,1024]{2,1,0:T(8,128)(2,1)} %states.1, bf16[128,1024]{1,0:T(8,128)(2,1)} %final.1, s32[8]{0:T(128)} %retained.1, s32[8]{0:T(128)} %slot.1, bf16[1,1024,1024]{2,1,0:T(8,128)(2,1)} %w_in.1, ...), custom_call_target="tpu_custom_call" | custom-call | tf_op jit(solution)/shard_map/distill/pallas_call | solution.py:671
  117.6 4.5 %last.1 = (bf16[1,192,1024]{2,1,0:T(8,128)(2,1)}, bf16[1,1024,1024]{2,1,0:T(8,128)(2,1)}, bf16[1,1024,1024]{2,1,0:T(8,128)(2,1)}, f32[1]{0:T(128)}) custom-call(bf16[192,1024]{1,0:T(8,128)(2,1)} %get-tuple-element.12.side, bf16[1024,1024]{1,0:T(8,128)(2,1)} %get-tuple-element.13.out, bf16[1024,1024]{1,0:T(8,128)(2,1)} %get-tuple-element.14.inn, ...), custom_call_target="tpu_custom_call" | custom-call | tf_op jit(solution)/shard_map/last/pallas_call | solution.py:687
